TPU v7x, 128 devices: a whole 4x4x4 slice. The times are simulated.
128 devices in a mesh: grp: 16 (over x, y), tp: 8 (over z, core).
Axes of the slice: x: 4, y: 4, z: 4, core: 2. Of those that a mesh axis runs over, the one named last changes fastest.
Arguments:
- queries: bfloat16 [32, 64, 256, 128], P('grp', 'tp'), may hold values from -8 to 8
- new_kv: bfloat16 [32, 8, 256, 256], P('grp', 'tp'), may hold values from -4.5 to 4.5
- kv_pool: bfloat16 [2048, 8, 128, 256], P(('grp', 'tp')), may hold values from -4.5 to 4.5
- cache_lens: int32 [32], replicated, may hold values from 1 to 7936, 126976 in all
- session_seat: int32 [32], replicated, may hold values from 0 to 31, as said below
- old_slots: int32 [32, 64], replicated, may hold values from 0 to 2047, as said below
- new_slots: int32 [32, 64], replicated, may hold values from 0 to 2047, as said below
Outputs:
- attention: bfloat16 [32, 64, 256, 128], P('grp', 'tp')
- new_pool: bfloat16 [2048, 8, 128, 256], P(('grp', 'tp'))
Inputs may be any that keep to these rules, and one draw needn't show every extreme that they name: `session_seat`: A permutation of the sessions. `old_slots`: every pool block appears exactly once. Call the group of session s session_seat[s] // 2; every device of grp+tp holds exactly 1 of its 16 blocks for the sessions of each group. `new_slots`: every pool block appears exactly once, and every device holds exactly 1 block for the sessions of each group, as for old_slots.
All inputs are finite; a program needn't handle non-finite values.
Results may differ from a plain program's by a relative error of at most 0.005.
Values may be sent and summed in bfloat16 or wider, within the bound.
No kernel may reach another device: no remote copies, remote signals or barrier semaphores. Data moves between devices by JAX's collectives and lax.ppermute only.
A program may use at most 128 MiB of HBM per device.

v0:
```python
import functools
import math

import jax
import jax.numpy as jnp
from jax import lax
from jax.experimental import pallas as pl
from jax.experimental.pallas import tpu as pltpu
from jax.sharding import PartitionSpec as P

MASKED = -1e30
CHUNK_BLOCKS = 8


def pack_kernel(code_ref, pool_ref, out_ref, held, load_sems, store_sems):
    count = out_ref.shape[0]

    def load(g):
        slot = lax.rem(code_ref[g], count)
        return pltpu.make_async_copy(pool_ref.at[slot], held.at[g], load_sems.at[g])

    def store(g):
        return pltpu.make_async_copy(held.at[g], out_ref.at[g], store_sems.at[g])

    def forward(g):
        load(g).wait()
        store(g).start()

    for g in range(count):
        pl.when(code_ref[g] >= count)(lambda g=g: load(g).start())
    for g in range(count):
        pl.when(code_ref[g] >= count)(lambda g=g: forward(g))
    for g in range(count):
        pl.when(code_ref[g] >= count)(lambda g=g: store(g).wait())


def unpack_kernel(code_ref, arrived_ref, out_ref, held, zeros, load_sems, store_sems):
    count = out_ref.shape[0]

    def load(g):
        return pltpu.make_async_copy(arrived_ref.at[g], held.at[g], load_sems.at[g])

    def store(g, source):
        slot = lax.rem(code_ref[g], count)
        return pltpu.make_async_copy(source, out_ref.at[slot], store_sems.at[g])

    def forward(g):
        load(g).wait()
        store(g, held.at[g]).start()

    for g in range(count):
        pl.when(code_ref[g] >= count)(lambda g=g: load(g).start())
    zeros[...] = jnp.zeros_like(zeros)
    for g in range(count):
        pl.when(code_ref[g] < count)(lambda g=g: store(g, zeros).start())
    for g in range(count):
        pl.when(code_ref[g] >= count)(lambda g=g: forward(g))
    for g in range(count):
        store(g, zeros).wait()


def grow_kernel(
    src_ref, dst_ref, lens_ref, fresh_ref, recv_ref, out_ref,
    held, edge_in, edge_out, load_sems, store_sems, edge_sems,
):
    seats, max_blocks = src_ref.shape
    block_len = recv_ref.shape[1]
    turn = fresh_ref.shape[1]
    spill = turn // block_len + 1

    def load(q, j):
        return pltpu.make_async_copy(recv_ref.at[src_ref[q, j]], held.at[q, j], load_sems.at[q, j])

    def store(q, j):
        return pltpu.make_async_copy(held.at[q, j], out_ref.at[dst_ref[q, j]], store_sems.at[q, j])

    def forward(q, j):
        load(q, j).wait()
        store(q, j).start()

    def edge_load(q):
        edge = lens_ref[q] // block_len
        return pltpu.make_async_copy(recv_ref.at[src_ref[q, edge]], edge_in.at[q], edge_sems.at[q, 0])

    def edge_store(q, k):
        edge = lens_ref[q] // block_len
        return pltpu.make_async_copy(
            edge_out.at[q, pl.ds(k * block_len, block_len)],
            out_ref.at[dst_ref[q, edge + k]],
            edge_sems.at[q, 1 + k],
        )

    for q in range(seats):
        edge_load(q).start()
    for q in range(seats):
        pl.loop(0, lens_ref[q] // block_len)(lambda j, q=q: load(q, j).start())
    for q in range(seats):
        pl.loop(0, lens_ref[q] // block_len)(lambda j, q=q: forward(q, j))
    for q in range(seats):
        rest = lens_ref[q] % block_len
        fresh = fresh_ref[q].astype(jnp.float32)
        tail = jnp.zeros((block_len, fresh.shape[1]), jnp.float32)
        moved = pltpu.roll(jnp.concatenate([fresh, tail], axis=0), rest, 0)
        edge_load(q).wait()
        row = lax.broadcasted_iota(jnp.int32, (block_len, fresh.shape[1]), 0)
        first = jnp.where(row < rest, edge_in[q].astype(jnp.float32), moved[:block_len])
        edge_out[q, :block_len] = first.astype(edge_out.dtype)
        edge_out[q, block_len:] = moved[block_len:].astype(edge_out.dtype)
        for k in range(spill - 1):
            edge_store(q, k).start()
        pl.when(rest > 0)(lambda q=q: edge_store(q, spill - 1).start())
    for q in range(seats):
        for k in range(spill - 1):
            edge_store(q, k).wait()
        rest = lens_ref[q] % block_len
        pl.when(rest > 0)(lambda q=q: edge_store(q, spill - 1).wait())
    for q in range(seats):
        pl.loop(0, lens_ref[q] // block_len)(lambda j, q=q: store(q, j).wait())


def attend_kernel(
    src_ref, lens_ref, queries_ref, fresh_ref, recv_ref, out_ref, cache, acc, high, sems
):
    seats, max_blocks = src_ref.shape
    block_len = recv_ref.shape[1]
    head_dim = queries_ref.shape[3]
    heads = queries_ref.shape[1]
    turn = queries_ref.shape[2]
    span = CHUNK_BLOCKS * block_len
    factor = head_dim ** (-0.5) * math.log2(math.e)
    pair = 2

    def row_copy(q, j):
        return pltpu.make_async_copy(
            recv_ref.at[src_ref[q, j]],
            cache.at[q, pl.ds(pl.multiple_of(j * block_len, block_len), block_len)],
            sems.at[q, j],
        )

    def blocks_of(q):
        return (lens_ref[q] + block_len - 1) // block_len

    def chunks_of(q):
        return (lens_ref[q] + span - 1) // span

    for q in range(seats):
        pl.loop(0, blocks_of(q))(lambda j, q=q: row_copy(q, j).start())

    def values_of(rows):
        ones = jnp.ones((rows.shape[0], head_dim), rows.dtype)
        return jnp.concatenate([rows[:, head_dim:], ones], axis=1)

    def score(query, rows):
        return (
            lax.dot_general(
                query, rows[:, :head_dim], (((1,), (1,)), ((), ())),
                preferred_element_type=jnp.float32,
            )
            * factor
        )

    def weigh(scores, top, rows):
        weights = jnp.exp2(scores - top).astype(jnp.bfloat16)
        return jnp.dot(weights, values_of(rows), preferred_element_type=jnp.float32)

    for q in range(seats):
        length = lens_ref[q]
        pl.loop(0, blocks_of(q))(lambda j, q=q: row_copy(q, j).wait())

        @pl.loop(blocks_of(q), chunks_of(q) * CHUNK_BLOCKS)
        def _(j, q=q):
            start = pl.multiple_of(j * block_len, block_len)
            cache[q, pl.ds(start, block_len)] = jnp.zeros((block_len, cache.shape[2]), cache.dtype)

        @pl.loop(0, heads // pair)
        def _(h, q=q, length=length):
            row = lax.broadcasted_iota(jnp.int32, (turn, turn), 0)
            column = lax.broadcasted_iota(jnp.int32, (turn, turn), 1)
            fresh = fresh_ref[q]
            for k in range(pair):
                scores = score(queries_ref[q, h * pair + k], fresh)
                scores = jnp.where(column <= row, scores, MASKED)
                top = jnp.max(scores, axis=1, keepdims=True)
                acc[k] = weigh(scores, top, fresh)
                high[k] = jnp.broadcast_to(top, high.shape[1:])

            def step(c, masked):
                start = pl.multiple_of(c * span, span)
                rows = cache[q, pl.ds(start, span)]
                for k in range(pair):
                    scores = score(queries_ref[q, h * pair + k], rows)
                    if masked:
                        position = start + lax.broadcasted_iota(jnp.int32, (1, span), 1)
                        scores = jnp.where(position < length, scores, MASKED)
                    old = high[k, :, :1]
                    top = jnp.maximum(old, jnp.max(scores, axis=1, keepdims=True))
                    acc[k] = acc[k] * jnp.exp2(old - top) + weigh(scores, top, rows)
                    high[k] = jnp.broadcast_to(top, high.shape[1:])

            full = length // span
            pl.loop(0, full)(lambda c: step(c, False))
            pl.when(length > full * span)(lambda: step(full, True))
            for k in range(pair):
                total = acc[k, :, head_dim : head_dim + 1]
                out_ref[q, h * pair + k] = (acc[k, :, :head_dim] / total).astype(out_ref.dtype)


def local(queries, new_kv, kv_pool, cache_lens, session_seat, old_slots, new_slots):
    group_count = lax.axis_size("grp")
    tp_count = lax.axis_size("tp")
    pool_dev, kv_heads, block_len, pair_width = kv_pool.shape
    seats_group, heads, turn, head_dim = queries.shape
    max_blocks = old_slots.shape[1]
    owners = group_count * tp_count
    assert pool_dev == group_count and kv_heads == tp_count
    group_index = lax.axis_index("grp")
    my_index = group_index * tp_count + lax.axis_index("tp")
    dtype = kv_pool.dtype
    any_space = pl.BlockSpec(memory_space=pl.ANY)
    vmem = pl.BlockSpec(memory_space=pltpu.VMEM)

    block_start = jnp.arange(max_blocks, dtype=jnp.int32)[None, :] * block_len
    session_group = session_seat // seats_group
    group_ids = jnp.arange(group_count, dtype=jnp.int32)

    def codes(slots, lengths):
        live = (block_start < lengths[:, None]).astype(jnp.int32)
        code = slots % pool_dev + pool_dev * live
        code = jnp.where(slots // pool_dev == my_index, code, 0)
        picked = jnp.where(session_group[None, :, None] == group_ids[:, None, None], code[None], 0)
        return jnp.sum(picked, axis=(1, 2))

    pack_codes = codes(old_slots, cache_lens)
    outgoing = pl.pallas_call(
        pack_kernel,
        grid_spec=pltpu.PrefetchScalarGridSpec(
            num_scalar_prefetch=1,
            grid=(1,),
            in_specs=[any_space],
            out_specs=any_space,
            scratch_shapes=[
                pltpu.VMEM((group_count, kv_heads, block_len, pair_width), dtype),
                pltpu.SemaphoreType.DMA((group_count,)),
                pltpu.SemaphoreType.DMA((group_count,)),
            ],
        ),
        out_shape=jax.ShapeDtypeStruct((group_count, kv_heads, block_len, pair_width), dtype),
        compiler_params=pltpu.CompilerParams(vmem_limit_bytes=16 * 1024 * 1024),
        name="pack",
    )(pack_codes, kv_pool)
    received = lax.all_to_all(
        outgoing.reshape(owners, block_len, pair_width),
        ("grp", "tp"), split_axis=0, concat_axis=0, tiled=True,
    )

    seat_ids = group_index * seats_group + jnp.arange(seats_group, dtype=jnp.int32)
    mine = (session_seat[None, :] == seat_ids[:, None]).astype(jnp.int32)
    my_lens = jnp.sum(mine * cache_lens[None, :], axis=1)
    my_old = jnp.sum(mine[:, :, None] * (old_slots // pool_dev)[None], axis=1)
    my_new = jnp.sum(mine[:, :, None] * (new_slots // pool_dev)[None], axis=1)
    unpack_codes = codes(new_slots, cache_lens + turn)
    fresh = new_kv.reshape(seats_group, turn, pair_width)

    spill = turn // block_len + 1
    leaving = pl.pallas_call(
        grow_kernel,
        grid_spec=pltpu.PrefetchScalarGridSpec(
            num_scalar_prefetch=3,
            grid=(1,),
            in_specs=[vmem, any_space],
            out_specs=any_space,
            scratch_shapes=[
                pltpu.VMEM((seats_group, max_blocks, block_len, pair_width), dtype),
                pltpu.VMEM((seats_group, block_len, pair_width), dtype),
                pltpu.VMEM((seats_group, spill * block_len, pair_width), dtype),
                pltpu.SemaphoreType.DMA((seats_group, max_blocks)),
                pltpu.SemaphoreType.DMA((seats_group, max_blocks)),
                pltpu.SemaphoreType.DMA((seats_group, 1 + spill)),
            ],
        ),
        out_shape=jax.ShapeDtypeStruct((owners, block_len, pair_width), dtype),
        compiler_params=pltpu.CompilerParams(vmem_limit_bytes=20 * 1024 * 1024),
        name="grow",
    )(my_old, my_new, my_lens, fresh, received)
    arrived = lax.all_to_all(leaving, ("grp", "tp"), split_axis=0, concat_axis=0, tiled=True)

    attention = pl.pallas_call(
        attend_kernel,
        grid_spec=pltpu.PrefetchScalarGridSpec(
            num_scalar_prefetch=2,
            grid=(1,),
            in_specs=[vmem, vmem, any_space],
            out_specs=vmem,
            scratch_shapes=[
                pltpu.VMEM((seats_group, max_blocks * block_len, pair_width), dtype),
                pltpu.VMEM((2, turn, 2 * head_dim), jnp.float32),
                pltpu.VMEM((2, turn, head_dim), jnp.float32),
                pltpu.SemaphoreType.DMA((seats_group, max_blocks)),
            ],
        ),
        out_shape=jax.ShapeDtypeStruct(queries.shape, dtype),
        compiler_params=pltpu.CompilerParams(vmem_limit_bytes=40 * 1024 * 1024),
        cost_estimate=pl.CostEstimate(
            flops=4 * seats_group * heads * turn * max_blocks * block_len * head_dim,
            bytes_accessed=owners * block_len * pair_width * 2,
            transcendentals=seats_group * heads * turn * max_blocks * block_len,
        ),
        name="attend",
    )(my_old, my_lens, queries, fresh, received)

    new_pool = pl.pallas_call(
        unpack_kernel,
        grid_spec=pltpu.PrefetchScalarGridSpec(
            num_scalar_prefetch=1,
            grid=(1,),
            in_specs=[any_space],
            out_specs=any_space,
            scratch_shapes=[
                pltpu.VMEM((group_count, kv_heads, block_len, pair_width), dtype),
                pltpu.VMEM((kv_heads, block_len, pair_width), dtype),
                pltpu.SemaphoreType.DMA((group_count,)),
                pltpu.SemaphoreType.DMA((group_count,)),
            ],
        ),
        out_shape=jax.ShapeDtypeStruct(kv_pool.shape, dtype),
        compiler_params=pltpu.CompilerParams(vmem_limit_bytes=16 * 1024 * 1024),
        name="unpack",
    )(unpack_codes, arrived.reshape(group_count, kv_heads, block_len, pair_width))
    return attention, new_pool


def solution(mesh):
    in_specs = (
        P("grp", "tp", None, None),
        P("grp", "tp", None, None),
        P(("grp", "tp"), None, None, None),
        P(),
        P(),
        P(),
        P(),
    )
    out_specs = (P("grp", "tp", None, None), P(("grp", "tp"), None, None, None))
    return jax.shard_map(local, mesh=mesh, in_specs=in_specs, out_specs=out_specs, check_vma=False)
```

profile of v0, /device:TPU:1, one launch (start us, length us, event | category | flops | bytes accessed | tf_op | source)
XLA Modules:
  0.0 261.1 jit_solution(3358997110335178660)
XLA Ops:
  0.6 0.7 broadcast_add_fusion
  1.3 0.7 and_select_fusion
  2.0 0.8 fusion.1
  2.8 0.8 select_reduce_fusion
  3.6 0.0 copy-start.2
  3.6 3.4 %copy-done.2 = bf16[16,8,128,256]{3,2,1,0:T(8,128)(2,1)S(1)} copy-done((bf16[16,8,128,256]{3,2,1,0:T(8,128)(2,1)S(1)}, bf16[16,8,128,256]{3,2,1,0:T(8,128)(2,1)}, u32[]{:S(2)}) %copy-start.2) | copy-done | bytes 8388632
  7.0 1.6 pack.1
  8.6 0.0 copy-start
  8.6 3.4 %copy-done = bf16[16,8,128,256]{3,2,1,0:T(8,128)(2,1)} copy-done((bf16[16,8,128,256]{3,2,1,0:T(8,128)(2,1)}, bf16[16,8,128,256]{3,2,1,0:T(8,128)(2,1)S(1)}, u32[]{:S(2)}) %copy-start) | copy-done | bytes 8388632
  12.0 0.0 copy-start.5
  12.0 0.0 copy-start.6
  12.0 0.0 copy-start.3
  12.0 12.1 %all-to-all-start = ((bf16[128,128,256]{2,1,0:T(8,128)(2,1)}), bf16[128,128,256]{2,1,0:T(8,128)(2,1)}, u32[]{:S(2)}, u32[]{:S(2)}) async-start(bf16[128,128,256]{2,1,0:T(8,128)(2,1)} %bitcast.3), calls=%async_computation | async-start | bytes 16777216 | tf_op jit(solution)/shard_map/all_to_all | solution.py:251
  24.1 0.0 copy-done.5
  24.1 0.0 copy-done.6
  24.1 0.2 fusion.8.lens_ref
  24.3 0.1 compare_convert_fusion
  24.4 0.1 multiply_reduce_fusion
  24.5 102.2 %all-to-all-done.recv_ref = bf16[128,128,256]{2,1,0:T(8,128)(2,1)} async-done(((bf16[128,128,256]{2,1,0:T(8,128)(2,1)}), bf16[128,128,256]{2,1,0:T(8,128)(2,1)}, u32[]{:S(2)}, u32[]{:S(2)}) %all-to-all-start) | async-done | bytes 8388640 | tf_op jit(solution)/shard_map/all_to_all | solution.py:251
  126.7 0.0 copy-done.3
  126.7 13.1 %grow.1 = bf16[128,128,256]{2,1,0:T(8,128)(2,1)S(1)} custom-call(s32[2,64]{1,0:T(2,128)S(1)} %get-tuple-element.5.src_ref, s32[2,64]{1,0:T(2,128)S(1)} %get-tuple-element.4.dst_ref, s32[2]{0:T(128)S(1)} %fusion.8.lens_ref, bf16[2,256,256]{2,1,0:T(8,128)(2,1)S(1)} %bitcast.4, bf16[128,128,256]{2,1,0:T(8,128)(2,1)} %all-to-all-done.recv_ref), custom_call_target="tpu_custom_call" | custom-call | tf_op jit(solution)/shard_map/grow/pallas_call | solution.py:265
  139.9 0.0 copy-start.1
  139.9 3.4 %copy-done.1 = bf16[128,128,256]{2,1,0:T(8,128)(2,1)} copy-done((bf16[128,128,256]{2,1,0:T(8,128)(2,1)}, bf16[128,128,256]{2,1,0:T(8,128)(2,1)S(1)}, u32[]{:S(2)}) %copy-start.1) | copy-done | bytes 8388632
  143.3 0.0 copy-start.4
  143.3 8.8 %all-to-all-start.1 = ((bf16[128,128,256]{2,1,0:T(8,128)(2,1)}), bf16[128,128,256]{2,1,0:T(8,128)(2,1)}, u32[]{:S(2)}, u32[]{:S(2)}) async-start(bf16[128,128,256]{2,1,0:T(8,128)(2,1)} %copy-done.1), calls=%async_computation.1 | async-start | bytes 16777216 | tf_op jit(solution)/shard_map/all_to_all | solution.py:285
  152.1 0.0 copy-done.4
  152.1 66.3 %attend.1 = bf16[2,8,256,128]{3,2,1,0:T(8,128)(2,1)} custom-call(s32[2,64]{1,0:T(2,128)S(1)} %get-tuple-element.5.src_ref, s32[2]{0:T(128)S(1)} %fusion.8.lens_ref, bf16[2,8,256,128]{3,2,1,0:T(8,128)(2,1)S(1)} %copy-done.4, bf16[2,256,256]{2,1,0:T(8,128)(2,1)S(1)} %bitcast.5, bf16[128,128,256]{2,1,0:T(8,128)(2,1)} %all-to-all-done.recv_ref), custom_call_target="tpu_custom_call" | custom-call | flops 17179869184 | bytes 8388608 | tf_op jit(solution)/shard_map/attend/pallas_call | solution.py:287
  218.4 36.3 %all-to-all-done.1 = bf16[128,128,256]{2,1,0:T(8,128)(2,1)} async-done(((bf16[128,128,256]{2,1,0:T(8,128)(2,1)}), bf16[128,128,256]{2,1,0:T(8,128)(2,1)}, u32[]{:S(2)}, u32[]{:S(2)}) %all-to-all-start.1) | async-done | bytes 8388640 | tf_op jit(solution)/shard_map/all_to_all | solution.py:285
  254.7 6.4 %unpack.1 = bf16[16,8,128,256]{3,2,1,0:T(8,128)(2,1)} custom-call(s32[16]{0:T(128)S(1)} %get-tuple-element.2.code_ref, bf16[16,8,128,256]{3,2,1,0:T(8,128)(2,1)} %bitcast.2.arrived_ref), custom_call_target="tpu_custom_call" | custom-call | tf_op jit(solution)/shard_map/unpack/pallas_call | solution.py:311
  (3 shorter events, 0.0 us)
Async XLA Ops:
  3.6 3.4 %copy-start.2 = (bf16[16,8,128,256]{3,2,1,0:T(8,128)(2,1)S(1)}, bf16[16,8,128,256]{3,2,1,0:T(8,128)(2,1)}, u32[]{:S(2)}) copy-start(bf16[16,8,128,256]{3,2,1,0:T(8,128)(2,1)} %pool_ref.1) | copy-start | bytes 25165828
  8.6 3.4 %copy-start = (bf16[16,8,128,256]{3,2,1,0:T(8,128)(2,1)}, bf16[16,8,128,256]{3,2,1,0:T(8,128)(2,1)S(1)}, u32[]{:S(2)}) copy-start(bf16[16,8,128,256]{3,2,1,0:T(8,128)(2,1)S(1)} %pack.1) | copy-start | bytes 25165828
  12.0 12.1 %copy-start.5 = (s32[32]{0:T(128)S(1)}, s32[32]{0:T(128)}, u32[]{:S(2)}) copy-start(s32[32]{0:T(128)} %param.10) | copy-start | bytes 388
  12.0 12.1 %copy-start.6 = (s32[32]{0:T(128)S(1)}, s32[32]{0:T(128)}, u32[]{:S(2)}) copy-start(s32[32]{0:T(128)} %param.11) | copy-start | bytes 388
  12.0 114.7 %copy-start.3 = (bf16[2,1,256,256]{3,2,1,0:T(8,128)(2,1)S(1)}, bf16[2,1,256,256]{3,2,1,0:T(8,128)(2,1)}, u32[]{:S(2)}) copy-start(bf16[2,1,256,256]{3,2,1,0:T(8,128)(2,1)} %param.8) | copy-start | bytes 786436
  12.0 114.7 %all-to-all-start = ((bf16[128,128,256]{2,1,0:T(8,128)(2,1)}), bf16[128,128,256]{2,1,0:T(8,128)(2,1)}, u32[]{:S(2)}, u32[]{:S(2)}) async-start(bf16[128,128,256]{2,1,0:T(8,128)(2,1)} %bitcast.3), calls=%async_computation | async-start | bytes 16777216 | tf_op jit(solution)/shard_map/all_to_all | solution.py:251
  139.9 3.4 %copy-start.1 = (bf16[128,128,256]{2,1,0:T(8,128)(2,1)}, bf16[128,128,256]{2,1,0:T(8,128)(2,1)S(1)}, u32[]{:S(2)}) copy-start(bf16[128,128,256]{2,1,0:T(8,128)(2,1)S(1)} %grow.1) | copy-start | bytes 25165828
  143.3 8.8 %copy-start.4 = (bf16[2,8,256,128]{3,2,1,0:T(8,128)(2,1)S(1)}, bf16[2,8,256,128]{3,2,1,0:T(8,128)(2,1)}, u32[]{:S(2)}) copy-start(bf16[2,8,256,128]{3,2,1,0:T(8,128)(2,1)} %queries_ref.1) | copy-start | bytes 3145732
  143.3 111.4 %all-to-all-start.1 = ((bf16[128,128,256]{2,1,0:T(8,128)(2,1)}), bf16[128,128,256]{2,1,0:T(8,128)(2,1)}, u32[]{:S(2)}, u32[]{:S(2)}) async-start(bf16[128,128,256]{2,1,0:T(8,128)(2,1)} %copy-done.1), calls=%async_computation.1 | async-start | bytes 16777216 | tf_op jit(solution)/shard_map/all_to_all | solution.py:285
where the time goes:
time: 266 us; the launch traced here: 261 us
  waiting for transfers between devices  139 us (52%)
  Pallas kernels  87.4 us (33%)
  starting transfers between devices  20.9 us (8%)
  local copies, waits for them, and re-layouts  10.2 us (4%)
  other arithmetic  3.31 us (1%)
    all_to_all x1, waiting for transfers between devices, local(): lax.all_to_all(outgoing.reshape(owners, block_len, pair_width), ('grp', '...  102 us
    pallas_call x1, Pallas kernels, local(): pl.pallas_call(attend_kernel, grid_spec=pltpu.PrefetchScalarGridSpec(num_...  66.3 us
    all_to_all x1, waiting for transfers between devices, local(): lax.all_to_all(leaving, ('grp', 'tp'), split_axis=0, concat_axis=0, tiled...  36.3 us
    pallas_call x1, Pallas kernels, local(): pl.pallas_call(grow_kernel, grid_spec=pltpu.PrefetchScalarGridSpec(num_sc...  13.1 us
    all_to_all x1, starting transfers between devices, local(): lax.all_to_all(outgoing.reshape(owners, block_len, pair_width), ('grp', '...  12.1 us
    unnamed x14, local copies, waits for them, and re-layouts  10.2 us
    all_to_all x1, starting transfers between devices, local(): lax.all_to_all(leaving, ('grp', 'tp'), split_axis=0, concat_axis=0, tiled...  8.8 us
    pallas_call x1, Pallas kernels, local(): pl.pallas_call(unpack_kernel, grid_spec=pltpu.PrefetchScalarGridSpec(num_...  6.38 us
  transfers between devices with their start and end apart: 2, of which 2 were waited for; matrix products, arithmetic and copies ran while one was open for 0% of the time, Pallas kernels for 25%

commit v1 on v0

--- a/solution.py
+++ b/solution.py
@@ -12,26 +12,39 @@
 CHUNK_BLOCKS = 8
 
 
-def pack_kernel(code_ref, pool_ref, out_ref, held, load_sems, store_sems):
-    count = out_ref.shape[0]
-
-    def load(g):
-        slot = lax.rem(code_ref[g], count)
-        return pltpu.make_async_copy(pool_ref.at[slot], held.at[g], load_sems.at[g])
-
-    def store(g):
-        return pltpu.make_async_copy(held.at[g], out_ref.at[g], store_sems.at[g])
-
-    def forward(g):
-        load(g).wait()
-        store(g).start()
-
-    for g in range(count):
-        pl.when(code_ref[g] >= count)(lambda g=g: load(g).start())
-    for g in range(count):
-        pl.when(code_ref[g] >= count)(lambda g=g: forward(g))
-    for g in range(count):
-        pl.when(code_ref[g] >= count)(lambda g=g: store(g).wait())
+def pack_kernel(slots_ref, seats_ref, lens_ref, pool_ref, out_ref, held, load_sems, store_sems, *, seats):
+    count, tp_count, block_len = pool_ref.shape[:3]
+    sessions, max_blocks = slots_ref.shape
+
+    def load(i):
+        return pltpu.make_async_copy(pool_ref.at[i], held.at[i], load_sems.at[i])
+
+    def store(i, g):
+        return pltpu.make_async_copy(held.at[i], out_ref.at[g], store_sems.at[i])
+
+    for i in range(count):
+        load(i).start()
+    square = (sessions, sessions)
+    diagonal = lax.broadcasted_iota(jnp.int32, square, 0) == lax.broadcasted_iota(jnp.int32, square, 1)
+
+    def column(row):
+        return jnp.sum(jnp.where(diagonal, row, 0), axis=1, keepdims=True)
+
+    group = lax.div(column(seats_ref[...]), seats)
+    start = lax.broadcasted_iota(jnp.int32, (sessions, max_blocks), 1) * block_len
+    code = jnp.where(start < column(lens_ref[...]), group + 1, 0)
+    my_index = lax.axis_index("grp") * tp_count + lax.axis_index("tp")
+    slot = slots_ref[...] - my_index * count
+    codes = [jnp.sum(jnp.where(slot == i, code, 0)) for i in range(count)]
+
+    def forward(i):
+        load(i).wait()
+        pl.when(codes[i] > 0)(lambda: store(i, codes[i] - 1).start())
+
+    for i in range(count):
+        forward(i)
+    for i in range(count):
+        pl.when(codes[i] > 0)(lambda i=i: store(i, codes[i] - 1).wait())
 
 
 def unpack_kernel(code_ref, arrived_ref, out_ref, held, zeros, load_sems, store_sems):
@@ -60,62 +73,43 @@
 
 
 def grow_kernel(
-    src_ref, dst_ref, lens_ref, fresh_ref, recv_ref, out_ref,
-    held, edge_in, edge_out, load_sems, store_sems, edge_sems,
+    pick_ref, dst_ref, edge_ref, lens_ref, fresh_ref, recv_ref, out_ref,
+    held, edge_in, load_sems, store_sem, edge_sems,
 ):
-    seats, max_blocks = src_ref.shape
-    block_len = recv_ref.shape[1]
-    turn = fresh_ref.shape[1]
+    owners, block_len, width = recv_ref.shape
+    seats, turn = fresh_ref.shape[:2]
     spill = turn // block_len + 1
-
-    def load(q, j):
-        return pltpu.make_async_copy(recv_ref.at[src_ref[q, j]], held.at[q, j], load_sems.at[q, j])
-
-    def store(q, j):
-        return pltpu.make_async_copy(held.at[q, j], out_ref.at[dst_ref[q, j]], store_sems.at[q, j])
-
-    def forward(q, j):
-        load(q, j).wait()
-        store(q, j).start()
+    parts = load_sems.shape[0]
+    share = owners // parts
+
+    def load(c):
+        rows = pl.ds(c * share, share)
+        return pltpu.make_async_copy(recv_ref.at[rows], held.at[rows], load_sems.at[c])
 
     def edge_load(q):
-        edge = lens_ref[q] // block_len
-        return pltpu.make_async_copy(recv_ref.at[src_ref[q, edge]], edge_in.at[q], edge_sems.at[q, 0])
-
-    def edge_store(q, k):
-        edge = lens_ref[q] // block_len
-        return pltpu.make_async_copy(
-            edge_out.at[q, pl.ds(k * block_len, block_len)],
-            out_ref.at[dst_ref[q, edge + k]],
-            edge_sems.at[q, 1 + k],
-        )
+        return pltpu.make_async_copy(recv_ref.at[edge_ref[q]], edge_in.at[q], edge_sems.at[q])
 
     for q in range(seats):
         edge_load(q).start()
+    for c in range(parts):
+        load(c).start()
+    row = lax.broadcasted_iota(jnp.int32, (block_len, width), 0)
     for q in range(seats):
-        pl.loop(0, lens_ref[q] // block_len)(lambda j, q=q: load(q, j).start())
-    for q in range(seats):
-        pl.loop(0, lens_ref[q] // block_len)(lambda j, q=q: forward(q, j))
-    for q in range(seats):
-        rest = lens_ref[q] % block_len
-        fresh = fresh_ref[q].astype(jnp.float32)
-        tail = jnp.zeros((block_len, fresh.shape[1]), jnp.float32)
-        moved = pltpu.roll(jnp.concatenate([fresh, tail], axis=0), rest, 0)
+        rest = lax.rem(lens_ref[q], block_len)
+        tail = jnp.zeros((block_len, width), jnp.float32)
+        moved = jnp.concatenate([fresh_ref[q].astype(jnp.float32), tail], axis=0)
+        moved = pltpu.roll(moved, rest, 0)
         edge_load(q).wait()
-        row = lax.broadcasted_iota(jnp.int32, (block_len, fresh.shape[1]), 0)
         first = jnp.where(row < rest, edge_in[q].astype(jnp.float32), moved[:block_len])
-        edge_out[q, :block_len] = first.astype(edge_out.dtype)
-        edge_out[q, block_len:] = moved[block_len:].astype(edge_out.dtype)
-        for k in range(spill - 1):
-            edge_store(q, k).start()
-        pl.when(rest > 0)(lambda q=q: edge_store(q, spill - 1).start())
-    for q in range(seats):
-        for k in range(spill - 1):
-            edge_store(q, k).wait()
-        rest = lens_ref[q] % block_len
-        pl.when(rest > 0)(lambda q=q: edge_store(q, spill - 1).wait())
-    for q in range(seats):
-        pl.loop(0, lens_ref[q] // block_len)(lambda j, q=q: store(q, j).wait())
+        held[owners + q * spill] = first.astype(held.dtype)
+        for k in range(1, spill):
+            later = moved[k * block_len : (k + 1) * block_len]
+            held[owners + q * spill + k] = later.astype(held.dtype)
+    for c in range(parts):
+        load(c).wait()
+        for o in range(c * share, (c + 1) * share):
+            pltpu.make_async_copy(held.at[pick_ref[o]], out_ref.at[dst_ref[o]], store_sem).start()
+    pltpu.make_async_copy(held.at[pl.ds(0, owners)], out_ref, store_sem).wait()
 
 
 def attend_kernel(
@@ -216,7 +210,7 @@
     group_index = lax.axis_index("grp")
     my_index = group_index * tp_count + lax.axis_index("tp")
     dtype = kv_pool.dtype
-    any_space = pl.BlockSpec(memory_space=pl.ANY)
+    hbm = pl.BlockSpec(memory_space=pltpu.HBM)
     vmem = pl.BlockSpec(memory_space=pltpu.VMEM)
 
     block_start = jnp.arange(max_blocks, dtype=jnp.int32)[None, :] * block_len
@@ -230,24 +224,19 @@
         picked = jnp.where(session_group[None, :, None] == group_ids[:, None, None], code[None], 0)
         return jnp.sum(picked, axis=(1, 2))
 
-    pack_codes = codes(old_slots, cache_lens)
     outgoing = pl.pallas_call(
-        pack_kernel,
-        grid_spec=pltpu.PrefetchScalarGridSpec(
-            num_scalar_prefetch=1,
-            grid=(1,),
-            in_specs=[any_space],
-            out_specs=any_space,
-            scratch_shapes=[
-                pltpu.VMEM((group_count, kv_heads, block_len, pair_width), dtype),
-                pltpu.SemaphoreType.DMA((group_count,)),
-                pltpu.SemaphoreType.DMA((group_count,)),
-            ],
-        ),
+        functools.partial(pack_kernel, seats=seats_group),
+        in_specs=[vmem, vmem, vmem, hbm],
+        out_specs=hbm,
+        scratch_shapes=[
+            pltpu.VMEM((group_count, kv_heads, block_len, pair_width), dtype),
+            pltpu.SemaphoreType.DMA((group_count,)),
+            pltpu.SemaphoreType.DMA((group_count,)),
+        ],
         out_shape=jax.ShapeDtypeStruct((group_count, kv_heads, block_len, pair_width), dtype),
         compiler_params=pltpu.CompilerParams(vmem_limit_bytes=16 * 1024 * 1024),
         name="pack",
-    )(pack_codes, kv_pool)
+    )(old_slots, session_seat[None, :], cache_lens[None, :], kv_pool)
     received = lax.all_to_all(
         outgoing.reshape(owners, block_len, pair_width),
         ("grp", "tp"), split_axis=0, concat_axis=0, tiled=True,
@@ -262,26 +251,34 @@
     fresh = new_kv.reshape(seats_group, turn, pair_width)
 
     spill = turn // block_len + 1
+    edge = (my_lens // block_len)[:, None]
+    past = jnp.arange(max_blocks, dtype=jnp.int32)[None, :] - edge
+    edge_row = owners + jnp.arange(seats_group, dtype=jnp.int32)[:, None] * spill + past
+    pick = jnp.where(jnp.logical_and(past >= 0, past < spill), edge_row, my_old)
+    edge_old = jnp.sum(jnp.where(past == 0, my_old, 0), axis=1)
+    owner_ids = jnp.arange(owners, dtype=jnp.int32)
+    from_owner = my_old[None] == owner_ids[:, None, None]
+    pick_rows = jnp.sum(jnp.where(from_owner, pick[None], 0), axis=(1, 2))
+    new_owner = jnp.sum(jnp.where(from_owner, my_new[None], 0), axis=(1, 2))
     leaving = pl.pallas_call(
         grow_kernel,
         grid_spec=pltpu.PrefetchScalarGridSpec(
-            num_scalar_prefetch=3,
+            num_scalar_prefetch=4,
             grid=(1,),
-            in_specs=[vmem, any_space],
-            out_specs=any_space,
+            in_specs=[vmem, hbm],
+            out_specs=hbm,
             scratch_shapes=[
-                pltpu.VMEM((seats_group, max_blocks, block_len, pair_width), dtype),
+                pltpu.VMEM((owners + seats_group * spill, block_len, pair_width), dtype),
                 pltpu.VMEM((seats_group, block_len, pair_width), dtype),
-                pltpu.VMEM((seats_group, spill * block_len, pair_width), dtype),
-                pltpu.SemaphoreType.DMA((seats_group, max_blocks)),
-                pltpu.SemaphoreType.DMA((seats_group, max_blocks)),
-                pltpu.SemaphoreType.DMA((seats_group, 1 + spill)),
+                pltpu.SemaphoreType.DMA((8,)),
+                pltpu.SemaphoreType.DMA,
+                pltpu.SemaphoreType.DMA((seats_group,)),
             ],
         ),
         out_shape=jax.ShapeDtypeStruct((owners, block_len, pair_width), dtype),
         compiler_params=pltpu.CompilerParams(vmem_limit_bytes=20 * 1024 * 1024),
         name="grow",
-    )(my_old, my_new, my_lens, fresh, received)
+    )(pick_rows, new_owner, edge_old, my_lens, fresh, received)
     arrived = lax.all_to_all(leaving, ("grp", "tp"), split_axis=0, concat_axis=0, tiled=True)
 
     attention = pl.pallas_call(
@@ -289,7 +286,7 @@
         grid_spec=pltpu.PrefetchScalarGridSpec(
             num_scalar_prefetch=2,
             grid=(1,),
-            in_specs=[vmem, vmem, any_space],
+            in_specs=[vmem, vmem, hbm],
             out_specs=vmem,
             scratch_shapes=[
                 pltpu.VMEM((seats_group, max_blocks * block_len, pair_width), dtype),
@@ -313,8 +310,8 @@
         grid_spec=pltpu.PrefetchScalarGridSpec(
             num_scalar_prefetch=1,
             grid=(1,),
-            in_specs=[any_space],
-            out_specs=any_space,
+            in_specs=[hbm],
+            out_specs=hbm,
             scratch_shapes=[
                 pltpu.VMEM((group_count, kv_heads, block_len, pair_width), dtype),
                 pltpu.VMEM((kv_heads, block_len, pair_width), dtype),

time: 266 us -> 265 us (level)
    unnamed x14 -> x24, local copies, waits for them, and re-layouts: 10.2 us -> 12.2 us
where the time goes in v1:
time: 265 us; the launch traced here: 263 us
  waiting for transfers between devices  137 us (52%)
  Pallas kernels  89 us (34%)
  starting transfers between devices  22 us (8%)
  local copies, waits for them, and re-layouts  12.2 us (5%)
    all_to_all x1, waiting for transfers between devices, local(): lax.all_to_all(outgoing.reshape(owners, block_len, pair_width), ('grp', '...  102 us
    pallas_call x1, Pallas kernels, local(): pl.pallas_call(attend_kernel, grid_spec=pltpu.PrefetchScalarGridSpec(num_...  66.7 us
    all_to_all x1, waiting for transfers between devices, local(): lax.all_to_all(leaving, ('grp', 'tp'), split_axis=0, concat_axis=0, tiled...  35.4 us
    pallas_call x1, Pallas kernels, local(): pl.pallas_call(grow_kernel, grid_spec=pltpu.PrefetchScalarGridSpec(num_sc...  15 us
    unnamed x24, local copies, waits for them, and re-layouts  12.2 us
    all_to_all x1, starting transfers between devices, local(): lax.all_to_all(outgoing.reshape(owners, block_len, pair_width), ('grp', '...  12.1 us
    all_to_all x1, starting transfers between devices, local(): lax.all_to_all(leaving, ('grp', 'tp'), split_axis=0, concat_axis=0, tiled...  9.98 us
    pallas_call x1, Pallas kernels, local(): pl.pallas_call(unpack_kernel, grid_spec=pltpu.PrefetchScalarGridSpec(num_...  5.99 us
  transfers between devices with their start and end apart: 2, of which 2 were waited for; matrix products, arithmetic and copies ran while one was open for 0% of the time, Pallas kernels for 25%

profile of v1, /device:TPU:1, one launch (start us, length us, event | category | flops | bytes accessed | tf_op | source)
XLA Modules:
  0.0 262.5 jit_solution(5218513888567730357)
XLA Ops:
  0.6 0.0 copy-start.2
  0.6 3.4 %copy-done.2 = bf16[16,8,128,256]{3,2,1,0:T(8,128)(2,1)S(1)} copy-done((bf16[16,8,128,256]{3,2,1,0:T(8,128)(2,1)S(1)}, bf16[16,8,128,256]{3,2,1,0:T(8,128)(2,1)}, u32[]{:S(2)}) %copy-start.2) | copy-done | bytes 8388632
  4.0 0.0 copy-start.4
  4.0 0.7 copy-done.4
  4.7 0.0 copy-start.6
  4.7 0.7 copy-done.6
  5.4 0.0 copy-start.8
  5.4 0.7 copy-done.8
  6.0 1.4 pack.1
  7.4 0.0 copy-start
  7.4 3.4 %copy-done = bf16[16,8,128,256]{3,2,1,0:T(8,128)(2,1)} copy-done((bf16[16,8,128,256]{3,2,1,0:T(8,128)(2,1)}, bf16[16,8,128,256]{3,2,1,0:T(8,128)(2,1)S(1)}, u32[]{:S(2)}) %copy-start) | copy-done | bytes 8388632
  10.8 0.0 copy-start.7
  10.8 0.0 copy-start.9
  10.8 0.0 copy-start.5
  10.8 0.0 copy-start.11
  10.8 0.0 copy-start.3
  10.8 12.1 %all-to-all-start = ((bf16[128,128,256]{2,1,0:T(8,128)(2,1)}), bf16[128,128,256]{2,1,0:T(8,128)(2,1)}, u32[]{:S(2)}, u32[]{:S(2)}) async-start(bf16[128,128,256]{2,1,0:T(8,128)(2,1)} %bitcast.5), calls=%async_computation | async-start | bytes 16777216 | tf_op jit(solution)/shard_map/all_to_all | solution.py:240
  22.9 0.0 copy-done.7
  23.0 0.0 copy-done.9
  23.0 0.2 fusion.7.lens_ref
  23.2 0.1 compare_convert_fusion
  23.2 0.0 copy-done.5
  23.2 0.0 copy-done.11
  23.2 0.1 fusion.2
  23.3 0.1 multiply_reduce_fusion
  23.4 0.2 fusion.6
  23.6 0.1 select_reduce_fusion.1
  23.7 101.8 %all-to-all-done.recv_ref = bf16[128,128,256]{2,1,0:T(8,128)(2,1)} async-done(((bf16[128,128,256]{2,1,0:T(8,128)(2,1)}), bf16[128,128,256]{2,1,0:T(8,128)(2,1)}, u32[]{:S(2)}, u32[]{:S(2)}) %all-to-all-start) | async-done | bytes 8388640 | tf_op jit(solution)/shard_map/all_to_all | solution.py:240
  125.5 0.0 copy-done.3
  125.5 15.0 %grow.1 = bf16[128,128,256]{2,1,0:T(8,128)(2,1)S(1)} custom-call(s32[128]{0:T(128)S(1)} %get-tuple-element.3.pick_ref, s32[128]{0:T(128)S(1)} %get-tuple-element.2.dst_ref, s32[2]{0:T(128)S(1)} %get-tuple-element.8.edge_ref, s32[2]{0:T(128)S(1)} %fusion.7.lens_ref, bf16[2,256,256]{2,1,0:T(8,128)(2,1)S(1)} %bitcast.6, ...), custom_call_target="tpu_custom_call" | custom-call | tf_op jit(solution)/shard_map/grow/pallas_call | solution.py:263
  140.5 0.0 copy-start.1
  140.5 3.4 %copy-done.1 = bf16[128,128,256]{2,1,0:T(8,128)(2,1)} copy-done((bf16[128,128,256]{2,1,0:T(8,128)(2,1)}, bf16[128,128,256]{2,1,0:T(8,128)(2,1)S(1)}, u32[]{:S(2)}) %copy-start.1) | copy-done | bytes 8388632
  143.9 0.0 copy-start.10
  143.9 10.0 %all-to-all-start.1 = ((bf16[128,128,256]{2,1,0:T(8,128)(2,1)}), bf16[128,128,256]{2,1,0:T(8,128)(2,1)}, u32[]{:S(2)}, u32[]{:S(2)}) async-start(bf16[128,128,256]{2,1,0:T(8,128)(2,1)} %copy-done.1), calls=%async_computation.1 | async-start | bytes 16777216 | tf_op jit(solution)/shard_map/all_to_all | solution.py:282
  153.9 0.5 select_reduce_fusion.code_ref
  154.4 0.0 copy-done.10
  154.4 66.7 %attend.1 = bf16[2,8,256,128]{3,2,1,0:T(8,128)(2,1)} custom-call(s32[2,64]{1,0:T(2,128)S(1)} %get-tuple-element.5.src_ref, s32[2]{0:T(128)S(1)} %fusion.7.lens_ref, bf16[2,8,256,128]{3,2,1,0:T(8,128)(2,1)S(1)} %copy-done.10, bf16[2,256,256]{2,1,0:T(8,128)(2,1)S(1)} %bitcast.7, bf16[128,128,256]{2,1,0:T(8,128)(2,1)} %all-to-all-done.recv_ref), custom_call_target="tpu_custom_call" | custom-call | flops 17179869184 | bytes 8388608 | tf_op jit(solution)/shard_map/attend/pallas_call | solution.py:284
  221.2 35.4 %all-to-all-done.1 = bf16[128,128,256]{2,1,0:T(8,128)(2,1)} async-done(((bf16[128,128,256]{2,1,0:T(8,128)(2,1)}), bf16[128,128,256]{2,1,0:T(8,128)(2,1)}, u32[]{:S(2)}, u32[]{:S(2)}) %all-to-all-start.1) | async-done | bytes 8388640 | tf_op jit(solution)/shard_map/all_to_all | solution.py:282
  256.5 6.0 %unpack.1 = bf16[16,8,128,256]{3,2,1,0:T(8,128)(2,1)} custom-call(s32[16]{0:T(128)S(1)} %select_reduce_fusion.code_ref, bf16[16,8,128,256]{3,2,1,0:T(8,128)(2,1)} %bitcast.4.arrived_ref), custom_call_target="tpu_custom_call" | custom-call | tf_op jit(solution)/shard_map/unpack/pallas_call | solution.py:308
  (7 shorter events, 0.0 us)
Async XLA Ops:
  0.6 3.4 %copy-start.2 = (bf16[16,8,128,256]{3,2,1,0:T(8,128)(2,1)S(1)}, bf16[16,8,128,256]{3,2,1,0:T(8,128)(2,1)}, u32[]{:S(2)}) copy-start(bf16[16,8,128,256]{3,2,1,0:T(8,128)(2,1)} %pool_ref.1) | copy-start | bytes 25165828
  4.0 0.7 copy-start.4
  4.7 0.7 copy-start.6
  5.4 0.7 copy-start.8
  7.4 3.4 %copy-start = (bf16[16,8,128,256]{3,2,1,0:T(8,128)(2,1)}, bf16[16,8,128,256]{3,2,1,0:T(8,128)(2,1)S(1)}, u32[]{:S(2)}) copy-start(bf16[16,8,128,256]{3,2,1,0:T(8,128)(2,1)S(1)} %pack.1) | copy-start | bytes 25165828
  10.8 12.1 %copy-start.7 = (s32[32]{0:T(128)S(1)}, s32[32]{0:T(128)}, u32[]{:S(2)}) copy-start(s32[32]{0:T(128)} %param.11) | copy-start | bytes 388
  10.8 12.1 %copy-start.9 = (s32[32]{0:T(128)S(1)}, s32[32]{0:T(128)}, u32[]{:S(2)}) copy-start(s32[32]{0:T(128)} %param.10) | copy-start | bytes 388
  10.8 12.4 %copy-start.5 = (s32[32,64]{1,0:T(8,128)S(1)}, s32[32,64]{1,0:T(8,128)}, u32[]{:S(2)}) copy-start(s32[32,64]{1,0:T(8,128)} %slots_ref.1) | copy-start | bytes 24580
  10.8 12.4 %copy-start.11 = (s32[32,64]{1,0:T(8,128)S(1)}, s32[32,64]{1,0:T(8,128)}, u32[]{:S(2)}) copy-start(s32[32,64]{1,0:T(8,128)} %param.13) | copy-start | bytes 24580
  10.8 114.7 %copy-start.3 = (bf16[2,1,256,256]{3,2,1,0:T(8,128)(2,1)S(1)}, bf16[2,1,256,256]{3,2,1,0:T(8,128)(2,1)}, u32[]{:S(2)}) copy-start(bf16[2,1,256,256]{3,2,1,0:T(8,128)(2,1)} %param.8) | copy-start | bytes 786436
  10.8 114.7 %all-to-all-start = ((bf16[128,128,256]{2,1,0:T(8,128)(2,1)}), bf16[128,128,256]{2,1,0:T(8,128)(2,1)}, u32[]{:S(2)}, u32[]{:S(2)}) async-start(bf16[128,128,256]{2,1,0:T(8,128)(2,1)} %bitcast.5), calls=%async_computation | async-start | bytes 16777216 | tf_op jit(solution)/shard_map/all_to_all | solution.py:240
  140.5 3.4 %copy-start.1 = (bf16[128,128,256]{2,1,0:T(8,128)(2,1)}, bf16[128,128,256]{2,1,0:T(8,128)(2,1)S(1)}, u32[]{:S(2)}) copy-start(bf16[128,128,256]{2,1,0:T(8,128)(2,1)S(1)} %grow.1) | copy-start | bytes 25165828
  143.9 10.5 %copy-start.10 = (bf16[2,8,256,128]{3,2,1,0:T(8,128)(2,1)S(1)}, bf16[2,8,256,128]{3,2,1,0:T(8,128)(2,1)}, u32[]{:S(2)}) copy-start(bf16[2,8,256,128]{3,2,1,0:T(8,128)(2,1)} %queries_ref.1) | copy-start | bytes 3145732
  143.9 112.6 %all-to-all-start.1 = ((bf16[128,128,256]{2,1,0:T(8,128)(2,1)}), bf16[128,128,256]{2,1,0:T(8,128)(2,1)}, u32[]{:S(2)}, u32[]{:S(2)}) async-start(bf16[128,128,256]{2,1,0:T(8,128)(2,1)} %copy-done.1), calls=%async_computation.1 | async-start | bytes 16777216 | tf_op jit(solution)/shard_map/all_to_all | solution.py:282

commit v2 on v1

--- a/solution.py
+++ b/solution.py
@@ -10,6 +10,7 @@
 
 MASKED = -1e30
 CHUNK_BLOCKS = 8
+VMEM_LIMIT = 60 * 1024 * 1024
 
 
 def pack_kernel(slots_ref, seats_ref, lens_ref, pool_ref, out_ref, held, load_sems, store_sems, *, seats):
@@ -234,7 +235,7 @@
             pltpu.SemaphoreType.DMA((group_count,)),
         ],
         out_shape=jax.ShapeDtypeStruct((group_count, kv_heads, block_len, pair_width), dtype),
-        compiler_params=pltpu.CompilerParams(vmem_limit_bytes=16 * 1024 * 1024),
+        compiler_params=pltpu.CompilerParams(vmem_limit_bytes=VMEM_LIMIT),
         name="pack",
     )(old_slots, session_seat[None, :], cache_lens[None, :], kv_pool)
     received = lax.all_to_all(
@@ -276,7 +277,7 @@
             ],
         ),
         out_shape=jax.ShapeDtypeStruct((owners, block_len, pair_width), dtype),
-        compiler_params=pltpu.CompilerParams(vmem_limit_bytes=20 * 1024 * 1024),
+        compiler_params=pltpu.CompilerParams(vmem_limit_bytes=VMEM_LIMIT),
         name="grow",
     )(pick_rows, new_owner, edge_old, my_lens, fresh, received)
     arrived = lax.all_to_all(leaving, ("grp", "tp"), split_axis=0, concat_axis=0, tiled=True)
@@ -296,7 +297,7 @@
             ],
         ),
         out_shape=jax.ShapeDtypeStruct(queries.shape, dtype),
-        compiler_params=pltpu.CompilerParams(vmem_limit_bytes=40 * 1024 * 1024),
+        compiler_params=pltpu.CompilerParams(vmem_limit_bytes=VMEM_LIMIT),
         cost_estimate=pl.CostEstimate(
             flops=4 * seats_group * heads * turn * max_blocks * block_len * head_dim,
             bytes_accessed=owners * block_len * pair_width * 2,
@@ -320,7 +321,7 @@
             ],
         ),
         out_shape=jax.ShapeDtypeStruct(kv_pool.shape, dtype),
-        compiler_params=pltpu.CompilerParams(vmem_limit_bytes=16 * 1024 * 1024),
+        compiler_params=pltpu.CompilerParams(vmem_limit_bytes=VMEM_LIMIT),
         name="unpack",
     )(unpack_codes, arrived.reshape(group_count, kv_heads, block_len, pair_width))
     return attention, new_pool

time: 265 us -> 251 us (0.947)
  local copies, waits for them, and re-layouts: 12.2 us -> 0.03 us
  Pallas kernels: 89 us -> 78.2 us
  waiting for transfers between devices: 137 us -> 144 us
    unnamed x24 -> x12, local copies, waits for them, and re-layouts: 12.2 us -> 0.03 us
    pallas_call x1, Pallas kernels: 66.7 us -> 57.9 us  [local(): pl.pallas_call(attend_kernel, grid_spec=pltpu.PrefetchScalarGridSpec(num_...]
    all_to_all x1, waiting for transfers between devices: 35.4 us -> 43.7 us  [local(): lax.all_to_all(leaving, ('grp', 'tp'), split_axis=0, concat_axis=0, tiled...]
    pallas_call x1, Pallas kernels: 15 us -> 7.99 us  [local(): pl.pallas_call(grow_kernel, grid_spec=pltpu.PrefetchScalarGridSpec(num_sc...]
    pallas_call x1, Pallas kernels: 1.37 us -> 6.27 us  [local(): pl.pallas_call(functools.partial(pack_kernel, seats=seats_group), in_spec...]
  transfers between devices with their start and end apart: 2 -> 2, of which waited for: 2 -> 2; matrix products, arithmetic and copies ran while one was open for 0% -> 1% of each run, Pallas kernels for 25% -> 23%
where the time goes in v2:
time: 251 us; the launch traced here: 248 us
  waiting for transfers between devices  144 us (57%)
  Pallas kernels  78.2 us (31%)
  starting transfers between devices  21.7 us (9%)
  other arithmetic  2.86 us (1%)
    all_to_all x1, waiting for transfers between devices, local(): lax.all_to_all(outgoing.reshape(owners, block_len, pair_width), ('grp', '...  101 us
    pallas_call x1, Pallas kernels, local(): pl.pallas_call(attend_kernel, grid_spec=pltpu.PrefetchScalarGridSpec(num_...  57.9 us
    all_to_all x1, waiting for transfers between devices, local(): lax.all_to_all(leaving, ('grp', 'tp'), split_axis=0, concat_axis=0, tiled...  43.7 us
    all_to_all x1, starting transfers between devices, local(): lax.all_to_all(outgoing.reshape(owners, block_len, pair_width), ('grp', '...  11.7 us
    all_to_all x1, starting transfers between devices, local(): lax.all_to_all(leaving, ('grp', 'tp'), split_axis=0, concat_axis=0, tiled...  9.99 us
    pallas_call x1, Pallas kernels, local(): pl.pallas_call(grow_kernel, grid_spec=pltpu.PrefetchScalarGridSpec(num_sc...  7.99 us
    pallas_call x1, Pallas kernels, local(): pl.pallas_call(functools.partial(pack_kernel, seats=seats_group), in_spec...  6.27 us
    pallas_call x1, Pallas kernels, local(): pl.pallas_call(unpack_kernel, grid_spec=pltpu.PrefetchScalarGridSpec(num_...  6.09 us
  transfers between devices with their start and end apart: 2, of which 2 were waited for; matrix products, arithmetic and copies ran while one was open for 1% of the time, Pallas kernels for 23%

profile of v2, /device:TPU:1, one launch (start us, length us, event | category | flops | bytes accessed | tf_op | source)
XLA Modules:
  0.0 248.0 jit_solution(12533557037948416671)
XLA Ops:
  0.6 6.3 %pack.1 = bf16[16,8,128,256]{3,2,1,0:T(8,128)(2,1)} custom-call(s32[32,64]{1,0:T(8,128)} %slots_ref.1, s32[1,32]{1,0:T(1,128)} %bitcast.8, s32[1,32]{1,0:T(1,128)} %bitcast.9, bf16[16,8,128,256]{3,2,1,0:T(8,128)(2,1)} %pool_ref.1), custom_call_target="tpu_custom_call" | custom-call | tf_op jit(solution)/shard_map/pack/pallas_call | solution.py:228
  6.9 0.0 copy-start.3
  6.9 0.0 copy-start.4
  6.9 0.0 copy-start
  6.9 0.0 copy-start.1
  7.0 11.7 %all-to-all-start = ((bf16[128,128,256]{2,1,0:T(8,128)(2,1)}), bf16[128,128,256]{2,1,0:T(8,128)(2,1)}, u32[]{:S(2)}, u32[]{:S(2)}) async-start(bf16[128,128,256]{2,1,0:T(8,128)(2,1)} %bitcast.5), calls=%async_computation | async-start | bytes 16777216 | tf_op jit(solution)/shard_map/all_to_all | solution.py:241
  18.7 0.0 copy-done.3
  18.7 0.0 copy-done.4
  18.7 0.2 fusion.7.lens_ref
  18.9 0.0 copy-start.5
  18.9 0.1 compare_convert_fusion
  19.0 0.0 copy-done
  19.0 0.0 copy-done.1
  19.0 0.1 fusion.2
  19.1 0.1 multiply_reduce_fusion
  19.2 0.0 copy-start.2
  19.2 0.7 fusion.6
  19.9 0.7 select_reduce_fusion.1
  20.6 100.7 %all-to-all-done.recv_ref = bf16[128,128,256]{2,1,0:T(8,128)(2,1)} async-done(((bf16[128,128,256]{2,1,0:T(8,128)(2,1)}), bf16[128,128,256]{2,1,0:T(8,128)(2,1)}, u32[]{:S(2)}, u32[]{:S(2)}) %all-to-all-start) | async-done | bytes 8388640 | tf_op jit(solution)/shard_map/all_to_all | solution.py:241
  121.3 0.0 copy-done.5
  121.3 8.0 %grow.1 = bf16[128,128,256]{2,1,0:T(8,128)(2,1)} custom-call(s32[128]{0:T(128)} %get-tuple-element.3.pick_ref, s32[128]{0:T(128)} %get-tuple-element.2.dst_ref, s32[2]{0:T(128)} %get-tuple-element.8.edge_ref, s32[2]{0:T(128)} %copy-done.5, bf16[2,256,256]{2,1,0:T(8,128)(2,1)} %bitcast.6, bf16[128,128,256]{2,1,0:T(8,128)(2,1)} %all-to-all-done.recv_ref), custom_call_target="tpu_custom_call" | custom-call | tf_op jit(solution)/shard_map/grow/pallas_call | solution.py:264
  129.3 0.0 copy-done.2
  129.3 10.0 %all-to-all-start.1 = ((bf16[128,128,256]{2,1,0:T(8,128)(2,1)}), bf16[128,128,256]{2,1,0:T(8,128)(2,1)}, u32[]{:S(2)}, u32[]{:S(2)}) async-start(bf16[128,128,256]{2,1,0:T(8,128)(2,1)} %grow.1), calls=%async_computation.1 | async-start | bytes 16777216 | tf_op jit(solution)/shard_map/all_to_all | solution.py:283
  139.3 1.0 select_reduce_fusion.code_ref
  140.4 57.9 %attend.1 = bf16[2,8,256,128]{3,2,1,0:T(8,128)(2,1)} custom-call(s32[2,64]{1,0:T(2,128)} %copy-done.2, s32[2]{0:T(128)} %copy-done.5, bf16[2,8,256,128]{3,2,1,0:T(8,128)(2,1)} %queries_ref.1, bf16[2,256,256]{2,1,0:T(8,128)(2,1)} %bitcast.7, bf16[128,128,256]{2,1,0:T(8,128)(2,1)} %all-to-all-done.recv_ref), custom_call_target="tpu_custom_call" | custom-call | flops 17179869184 | bytes 8388608 | tf_op jit(solution)/shard_map/attend/pallas_call | solution.py:285
  198.3 43.7 %all-to-all-done.1 = bf16[128,128,256]{2,1,0:T(8,128)(2,1)} async-done(((bf16[128,128,256]{2,1,0:T(8,128)(2,1)}), bf16[128,128,256]{2,1,0:T(8,128)(2,1)}, u32[]{:S(2)}, u32[]{:S(2)}) %all-to-all-start.1) | async-done | bytes 8388640 | tf_op jit(solution)/shard_map/all_to_all | solution.py:283
  241.9 6.1 %unpack.1 = bf16[16,8,128,256]{3,2,1,0:T(8,128)(2,1)} custom-call(s32[16]{0:T(128)} %select_reduce_fusion.code_ref, bf16[16,8,128,256]{3,2,1,0:T(8,128)(2,1)} %bitcast.4.arrived_ref), custom_call_target="tpu_custom_call" | custom-call | tf_op jit(solution)/shard_map/unpack/pallas_call | solution.py:309
  (7 shorter events, 0.0 us)
Async XLA Ops:
  6.9 11.8 %copy-start.3 = (s32[32]{0:T(128)S(1)}, s32[32]{0:T(128)}, u32[]{:S(2)}) copy-start(s32[32]{0:T(128)} %param.11) | copy-start | bytes 388
  6.9 11.8 %copy-start.4 = (s32[32]{0:T(128)S(1)}, s32[32]{0:T(128)}, u32[]{:S(2)}) copy-start(s32[32]{0:T(128)} %param.10) | copy-start | bytes 388
  6.9 12.1 %copy-start = (s32[32,64]{1,0:T(8,128)S(1)}, s32[32,64]{1,0:T(8,128)}, u32[]{:S(2)}) copy-start(s32[32,64]{1,0:T(8,128)} %slots_ref.1) | copy-start | bytes 24580
  6.9 12.1 %copy-start.1 = (s32[32,64]{1,0:T(8,128)S(1)}, s32[32,64]{1,0:T(8,128)}, u32[]{:S(2)}) copy-start(s32[32,64]{1,0:T(8,128)} %param.13) | copy-start | bytes 24580
  7.0 114.4 %all-to-all-start = ((bf16[128,128,256]{2,1,0:T(8,128)(2,1)}), bf16[128,128,256]{2,1,0:T(8,128)(2,1)}, u32[]{:S(2)}, u32[]{:S(2)}) async-start(bf16[128,128,256]{2,1,0:T(8,128)(2,1)} %bitcast.5), calls=%async_computation | async-start | bytes 16777216 | tf_op jit(solution)/shard_map/all_to_all | solution.py:241
  18.9 102.4 %copy-start.5 = (s32[2]{0:T(128)}, s32[2]{0:T(128)S(1)}, u32[]{:S(2)}) copy-start(s32[2]{0:T(128)S(1)} %fusion.7.lens_ref) | copy-start | bytes 28
  19.2 110.1 %copy-start.2 = (s32[2,64]{1,0:T(2,128)}, s32[2,64]{1,0:T(2,128)S(1)}, u32[]{:S(2)}) copy-start(s32[2,64]{1,0:T(2,128)S(1)} %get-tuple-element.5.src_ref) | copy-start | bytes 1540
  129.3 112.6 %all-to-all-start.1 = ((bf16[128,128,256]{2,1,0:T(8,128)(2,1)}), bf16[128,128,256]{2,1,0:T(8,128)(2,1)}, u32[]{:S(2)}, u32[]{:S(2)}) async-start(bf16[128,128,256]{2,1,0:T(8,128)(2,1)} %grow.1), calls=%async_computation.1 | async-start | bytes 16777216 | tf_op jit(solution)/shard_map/all_to_all | solution.py:283

commit v3 on v2

v3 whole, which is shorter than its diff:
```python
import functools
import math

import jax
import jax.numpy as jnp
from jax import lax
from jax.experimental import pallas as pl
from jax.experimental.pallas import tpu as pltpu
from jax.sharding import PartitionSpec as P

MASKED = -1e30
CHUNK_BLOCKS = 8
PICK, TARGET, LENGTHS, EDGES, CODES, SOURCES = range(6)
TABLE_ROWS = 8
VMEM_LIMIT = 60 * 1024 * 1024
PACK_LIMIT = 40 * 1024 * 1024


def pack_kernel(
    packed_ref, pool_ref, out_ref, table_ref, sems, *, seats, turn
):
    count, tp_count, block_len = pool_ref.shape[:3]
    sessions, max_blocks = packed_ref.shape[0], packed_ref.shape[1] // 2
    owners = table_ref.shape[1]
    spill = turn // block_len + 1
    my_group = lax.axis_index("grp")
    first_slot = (my_group * tp_count + lax.axis_index("tp")) * count

    shape = (sessions, max_blocks)
    block = lax.broadcasted_iota(jnp.int32, shape, 1)
    slots = owners * count
    old = lax.rem(packed_ref[:, :max_blocks], slots)
    new = lax.div(packed_ref[:, :max_blocks], slots)
    length = lax.div(packed_ref[:, max_blocks:], sessions)
    seat = lax.rem(packed_ref[:, max_blocks:], sessions)
    group = lax.div(seat, seats)

    def codes_of(slots, lengths):
        code = jnp.where(block * block_len < lengths, group + 1, 0)
        return [jnp.sum(jnp.where(slots - first_slot == i, code, 0)) for i in range(count)]

    codes = codes_of(old, length)

    def copy(i):
        return pltpu.make_async_copy(pool_ref.at[i], out_ref.at[codes[i] - 1], sems.at[i])

    for i in range(count):
        pl.when(codes[i] > 0)(lambda i=i: copy(i).start())

    table_ref[...] = jnp.zeros_like(table_ref)
    lane = lax.broadcasted_iota(jnp.int32, (1, owners), 1)
    code_row = jnp.zeros((1, owners), jnp.int32)
    for i, code in enumerate(codes_of(new, length + turn)):
        code_row = jnp.where(lane == i, code, code_row)
    table_ref[CODES : CODES + 1, :] = code_row

    square = (max_blocks, max_blocks)
    diagonal = lax.broadcasted_iota(jnp.int32, square, 0) == lax.broadcasted_iota(jnp.int32, square, 1)
    owner = lax.broadcasted_iota(jnp.int32, (max_blocks, owners), 1)
    place = lax.broadcasted_iota(jnp.int32, (1, max_blocks), 1)
    pick_row = jnp.zeros((1, owners), jnp.int32)
    target_row = jnp.zeros((1, owners), jnp.int32)
    length_row = jnp.zeros((1, owners), jnp.int32)
    edge_row = jnp.zeros((1, owners), jnp.int32)
    for q in range(seats):
        mine = seat == my_group * seats + q

        def of_seat(values):
            return jnp.sum(jnp.where(mine, values, 0), axis=0, keepdims=True)

        def column(row):
            return jnp.sum(jnp.where(diagonal, row, 0), axis=1, keepdims=True)

        my_length = of_seat(length)
        source = of_seat(lax.div(old, count))
        past = place - lax.div(my_length, block_len)
        on_edge = jnp.logical_and(past >= 0, past < spill)
        pick = jnp.where(on_edge, owners + q * spill + past, source)
        from_owner = owner == column(source)
        pick_row += jnp.sum(jnp.where(from_owner, column(pick), 0), axis=0, keepdims=True)
        target = column(of_seat(lax.div(new, count)))
        target_row += jnp.sum(jnp.where(from_owner, target, 0), axis=0, keepdims=True)
        edge = jnp.sum(jnp.where(past == 0, source, 0), axis=1, keepdims=True)
        edge_row = jnp.where(lane == q, edge, edge_row)
        length_row = jnp.where(lane == q, my_length[:, :1], length_row)
        table_ref[SOURCES + q : SOURCES + q + 1, :max_blocks] = source
    table_ref[PICK : PICK + 1, :] = pick_row
    table_ref[TARGET : TARGET + 1, :] = target_row
    table_ref[LENGTHS : LENGTHS + 1, :] = length_row
    table_ref[EDGES : EDGES + 1, :] = edge_row
    for i in range(count):
        pl.when(codes[i] > 0)(lambda i=i: copy(i).wait())


def unpack_kernel(table_ref, arrived_ref, out_ref, held, zeros, load_sems, store_sems):
    count = out_ref.shape[0]

    def load(i):
        source = arrived_ref.at[table_ref[CODES, i] - 1]
        return pltpu.make_async_copy(source, held.at[i], load_sems.at[i])

    def store(i, source):
        return pltpu.make_async_copy(source, out_ref.at[i], store_sems.at[i])

    def forward(i):
        load(i).wait()
        store(i, held.at[i]).start()

    for i in range(count):
        pl.when(table_ref[CODES, i] > 0)(lambda i=i: load(i).start())
    zeros[...] = jnp.zeros_like(zeros)
    for i in range(count):
        pl.when(table_ref[CODES, i] == 0)(lambda i=i: store(i, zeros).start())
    for i in range(count):
        pl.when(table_ref[CODES, i] > 0)(lambda i=i: forward(i))
    for i in range(count):
        store(i, zeros).wait()


def grow_kernel(
    table_ref, fresh_ref, recv_ref, out_ref,
    held, edge_in, load_sems, store_sem, edge_sems,
):
    owners, block_len, width = recv_ref.shape
    seats, turn = fresh_ref.shape[:2]
    spill = turn // block_len + 1
    parts = load_sems.shape[0]
    share = owners // parts

    def load(c):
        rows = pl.ds(c * share, share)
        return pltpu.make_async_copy(recv_ref.at[rows], held.at[rows], load_sems.at[c])

    def edge_load(q):
        return pltpu.make_async_copy(recv_ref.at[table_ref[EDGES, q]], edge_in.at[q], edge_sems.at[q])

    for q in range(seats):
        edge_load(q).start()
    for c in range(parts):
        load(c).start()
    row = lax.broadcasted_iota(jnp.int32, (block_len, width), 0)
    for q in range(seats):
        rest = lax.rem(table_ref[LENGTHS, q], block_len)
        tail = jnp.zeros((block_len, width), jnp.float32)
        moved = jnp.concatenate([fresh_ref[q].astype(jnp.float32), tail], axis=0)
        moved = pltpu.roll(moved, rest, 0)
        edge_load(q).wait()
        first = jnp.where(row < rest, edge_in[q].astype(jnp.float32), moved[:block_len])
        held[owners + q * spill] = first.astype(held.dtype)
        for k in range(1, spill):
            later = moved[k * block_len : (k + 1) * block_len]
            held[owners + q * spill + k] = later.astype(held.dtype)
    for c in range(parts):
        load(c).wait()
        for o in range(c * share, (c + 1) * share):
            row_in, row_out = held.at[table_ref[PICK, o]], out_ref.at[table_ref[TARGET, o]]
            pltpu.make_async_copy(row_in, row_out, store_sem).start()
    pltpu.make_async_copy(held.at[pl.ds(0, owners)], out_ref, store_sem).wait()


def attend_kernel(
    table_ref, queries_ref, fresh_ref, recv_ref, out_ref, cache, acc, high, sems
):
    seats = queries_ref.shape[0]
    block_len = recv_ref.shape[1]
    head_dim = queries_ref.shape[3]
    heads = queries_ref.shape[1]
    turn = queries_ref.shape[2]
    span = CHUNK_BLOCKS * block_len
    factor = head_dim ** (-0.5) * math.log2(math.e)
    pair = 2

    def row_copy(q, j):
        return pltpu.make_async_copy(
            recv_ref.at[table_ref[SOURCES + q, j]],
            cache.at[q, pl.ds(pl.multiple_of(j * block_len, block_len), block_len)],
            sems.at[q, j],
        )

    def blocks_of(q):
        return (table_ref[LENGTHS, q] + block_len - 1) // block_len

    def chunks_of(q):
        return (table_ref[LENGTHS, q] + span - 1) // span

    for q in range(seats):
        pl.loop(0, blocks_of(q))(lambda j, q=q: row_copy(q, j).start())

    def values_of(rows):
        ones = jnp.ones((rows.shape[0], head_dim), rows.dtype)
        return jnp.concatenate([rows[:, head_dim:], ones], axis=1)

    def score(query, rows):
        return (
            lax.dot_general(
                query, rows[:, :head_dim], (((1,), (1,)), ((), ())),
                preferred_element_type=jnp.float32,
            )
            * factor
        )

    def weigh(scores, top, rows):
        weights = jnp.exp2(scores - top).astype(jnp.bfloat16)
        return jnp.dot(weights, values_of(rows), preferred_element_type=jnp.float32)

    for q in range(seats):
        length = table_ref[LENGTHS, q]
        pl.loop(0, blocks_of(q))(lambda j, q=q: row_copy(q, j).wait())

        @pl.loop(blocks_of(q), chunks_of(q) * CHUNK_BLOCKS)
        def _(j, q=q):
            start = pl.multiple_of(j * block_len, block_len)
            cache[q, pl.ds(start, block_len)] = jnp.zeros((block_len, cache.shape[2]), cache.dtype)

        @pl.loop(0, heads // pair)
        def _(h, q=q, length=length):
            row = lax.broadcasted_iota(jnp.int32, (turn, turn), 0)
            column = lax.broadcasted_iota(jnp.int32, (turn, turn), 1)
            fresh = fresh_ref[q]
            for k in range(pair):
                scores = score(queries_ref[q, h * pair + k], fresh)
                scores = jnp.where(column <= row, scores, MASKED)
                top = jnp.max(scores, axis=1, keepdims=True)
                acc[k] = weigh(scores, top, fresh)
                high[k] = jnp.broadcast_to(top, high.shape[1:])

            def step(c, masked):
                start = pl.multiple_of(c * span, span)
                rows = cache[q, pl.ds(start, span)]
                for k in range(pair):
                    scores = score(queries_ref[q, h * pair + k], rows)
                    if masked:
                        position = start + lax.broadcasted_iota(jnp.int32, (1, span), 1)
                        scores = jnp.where(position < length, scores, MASKED)
                    old = high[k, :, :1]
                    top = jnp.maximum(old, jnp.max(scores, axis=1, keepdims=True))
                    acc[k] = acc[k] * jnp.exp2(old - top) + weigh(scores, top, rows)
                    high[k] = jnp.broadcast_to(top, high.shape[1:])

            full = length // span
            pl.loop(0, full)(lambda c: step(c, False))
            pl.when(length > full * span)(lambda: step(full, True))
            for k in range(pair):
                total = acc[k, :, head_dim : head_dim + 1]
                out_ref[q, h * pair + k] = (acc[k, :, :head_dim] / total).astype(out_ref.dtype)


def local(queries, new_kv, kv_pool, cache_lens, session_seat, old_slots, new_slots):
    group_count = lax.axis_size("grp")
    tp_count = lax.axis_size("tp")
    pool_dev, kv_heads, block_len, pair_width = kv_pool.shape
    seats_group, heads, turn, head_dim = queries.shape
    max_blocks = old_slots.shape[1]
    owners = group_count * tp_count
    assert pool_dev == group_count and kv_heads == tp_count and max_blocks <= owners
    dtype = kv_pool.dtype
    anywhere = pl.BlockSpec(memory_space=pl.ANY)
    vmem = pl.BlockSpec(memory_space=pltpu.VMEM)
    smem = pl.BlockSpec(memory_space=pltpu.SMEM)
    rows = jax.ShapeDtypeStruct((owners, block_len, pair_width), dtype)
    blocks = jax.ShapeDtypeStruct((group_count, kv_heads, block_len, pair_width), dtype)
    fresh = new_kv.reshape(seats_group, turn, pair_width)
    spill = turn // block_len + 1

    session = cache_lens * session_seat.shape[0] + session_seat
    packed = jnp.concatenate(
        [new_slots * (owners * pool_dev) + old_slots, jnp.broadcast_to(session[:, None], old_slots.shape)],
        axis=1,
    )
    outgoing, table = pl.pallas_call(
        functools.partial(pack_kernel, seats=seats_group, turn=turn),
        in_specs=[vmem, anywhere],
        out_specs=[anywhere, vmem],
        scratch_shapes=[pltpu.SemaphoreType.DMA((group_count,))],
        out_shape=[blocks, jax.ShapeDtypeStruct((TABLE_ROWS, owners), jnp.int32)],
        compiler_params=pltpu.CompilerParams(vmem_limit_bytes=PACK_LIMIT),
        name="pack",
    )(packed, kv_pool)
    received = lax.all_to_all(
        outgoing.reshape(rows.shape), ("grp", "tp"), split_axis=0, concat_axis=0, tiled=True
    )

    leaving = pl.pallas_call(
        grow_kernel,
        in_specs=[smem, vmem, anywhere],
        out_specs=anywhere,
        scratch_shapes=[
            pltpu.VMEM((owners + seats_group * spill, block_len, pair_width), dtype),
            pltpu.VMEM((seats_group, block_len, pair_width), dtype),
            pltpu.SemaphoreType.DMA((8,)),
            pltpu.SemaphoreType.DMA,
            pltpu.SemaphoreType.DMA((seats_group,)),
        ],
        out_shape=rows,
        compiler_params=pltpu.CompilerParams(vmem_limit_bytes=VMEM_LIMIT),
        name="grow",
    )(table, fresh, received)
    arrived = lax.all_to_all(leaving, ("grp", "tp"), split_axis=0, concat_axis=0, tiled=True)

    attention = pl.pallas_call(
        attend_kernel,
        in_specs=[smem, vmem, vmem, anywhere],
        out_specs=vmem,
        scratch_shapes=[
            pltpu.VMEM((seats_group, max_blocks * block_len, pair_width), dtype),
            pltpu.VMEM((2, turn, 2 * head_dim), jnp.float32),
            pltpu.VMEM((2, turn, head_dim), jnp.float32),
            pltpu.SemaphoreType.DMA((seats_group, max_blocks)),
        ],
        out_shape=jax.ShapeDtypeStruct(queries.shape, dtype),
        compiler_params=pltpu.CompilerParams(vmem_limit_bytes=VMEM_LIMIT),
        cost_estimate=pl.CostEstimate(
            flops=4 * seats_group * heads * turn * max_blocks * block_len * head_dim,
            bytes_accessed=owners * block_len * pair_width * 2,
            transcendentals=seats_group * heads * turn * max_blocks * block_len,
        ),
        name="attend",
    )(table, queries, fresh, received)

    new_pool = pl.pallas_call(
        unpack_kernel,
        in_specs=[smem, anywhere],
        out_specs=anywhere,
        scratch_shapes=[
            pltpu.VMEM(blocks.shape, dtype),
            pltpu.VMEM(blocks.shape[1:], dtype),
            pltpu.SemaphoreType.DMA((group_count,)),
            pltpu.SemaphoreType.DMA((group_count,)),
        ],
        out_shape=blocks,
        compiler_params=pltpu.CompilerParams(vmem_limit_bytes=VMEM_LIMIT),
        name="unpack",
    )(table, arrived.reshape(blocks.shape))
    return attention, new_pool


def solution(mesh):
    in_specs = (
        P("grp", "tp", None, None),
        P("grp", "tp", None, None),
        P(("grp", "tp"), None, None, None),
        P(),
        P(),
        P(),
        P(),
    )
    out_specs = (P("grp", "tp", None, None), P(("grp", "tp"), None, None, None))
    return jax.shard_map(local, mesh=mesh, in_specs=in_specs, out_specs=out_specs, check_vma=False)
```

time: 251 us -> 241 us (0.960)
  blocking collectives: 0 us -> 110 us
  waiting for transfers between devices: 144 us -> 66.9 us
  Pallas kernels: 78.2 us -> 51.7 us
  starting transfers between devices: 21.7 us -> 7.96 us
    all_to_all x0 -> x1, blocking collectives: none -> 110 us  [local(): lax.all_to_all(outgoing.reshape(rows.shape), ('grp', 'tp'), split_axis=0,...]
    all_to_all x1 -> x0, waiting for transfers between devices: 101 us -> none  [local(): lax.all_to_all(outgoing.reshape(owners, block_len, pair_width), ('grp', '...]
    pallas_call x4, Pallas kernels: 78.2 us -> 51.7 us  [the longest x1 35.7 us: local(): pl.pallas_call(attend_kernel, in_specs=[smem, vmem, vmem, anywhere], out_...]
    all_to_all x1, waiting for transfers between devices: 43.7 us -> 66.9 us  [local(): lax.all_to_all(leaving, ('grp', 'tp'), split_axis=0, concat_axis=0, tiled...]
    all_to_all x1 -> x0, starting transfers between devices: 11.7 us -> none  [local(): lax.all_to_all(outgoing.reshape(owners, block_len, pair_width), ('grp', '...]
    reduce_sum x5 -> x0, other arithmetic: 2.67 us -> none  [the longest x1 1.05 us: codes(): return jnp.sum(picked, axis=(1, 2))]
  transfers between devices with their start and end apart: 2 -> 1, of which waited for: 2 -> 1; matrix products, arithmetic and copies ran while one was open for 1% -> 0% of each run, Pallas kernels for 23% -> 15%
where the time goes in v3:
time: 241 us; the launch traced here: 239 us
  blocking collectives  110 us (46%)
  waiting for transfers between devices  66.9 us (28%)
  Pallas kernels  51.7 us (21%)
  starting transfers between devices  7.96 us (3%)
    all_to_all x1, blocking collectives, local(): lax.all_to_all(outgoing.reshape(rows.shape), ('grp', 'tp'), split_axis=0,...  110 us
    all_to_all x1, waiting for transfers between devices, local(): lax.all_to_all(leaving, ('grp', 'tp'), split_axis=0, concat_axis=0, tiled...  66.9 us
    pallas_call x1, Pallas kernels, local(): pl.pallas_call(attend_kernel, in_specs=[smem, vmem, vmem, anywhere], out_...  35.7 us
    all_to_all x1, starting transfers between devices, local(): lax.all_to_all(leaving, ('grp', 'tp'), split_axis=0, concat_axis=0, tiled...  7.96 us
    pallas_call x1, Pallas kernels, local(): pl.pallas_call(grow_kernel, in_specs=[smem, vmem, anywhere], out_specs=an...  7.31 us
    pallas_call x1, Pallas kernels, local(): pl.pallas_call(unpack_kernel, in_specs=[smem, anywhere], out_specs=anywhe...  6.17 us
  transfers between devices with their start and end apart: 1, of which 1 were waited for; matrix products, arithmetic and copies ran while one was open for 0% of the time, Pallas kernels for 15%

profile of v3, /device:TPU:1, one launch (start us, length us, event | category | flops | bytes accessed | tf_op | source)
XLA Modules:
  0.0 238.8 jit_solution(4985292057057896743)
XLA Ops:
  0.6 0.7 multiply_add_fusion.1
  1.3 0.7 multiply_add_fusion
  2.0 0.1 broadcast_in_dim.2
  2.1 0.1 pad_add_fusion.packed_ref
  2.2 2.5 %pack.1 = (bf16[16,8,128,256]{3,2,1,0:T(8,128)(2,1)S(1)}, s32[8,128]{1,0:T(8,128)S(1)}) custom-call(s32[32,128]{1,0:T(8,128)S(1)} %pad_add_fusion.packed_ref, bf16[16,8,128,256]{3,2,1,0:T(8,128)(2,1)} %pool_ref.1), custom_call_target="tpu_custom_call" | custom-call | tf_op jit(solution)/shard_map/pack/pallas_call | solution.py:270
  4.7 0.0 copy-start
  4.7 110.0 %all_to_all.10.recv_ref = bf16[128,128,256]{2,1,0:T(8,128)(2,1)} all-to-all(bf16[128,128,256]{2,1,0:T(8,128)(2,1)S(1)} %bitcast.3), channel_id=1, replica_groups=mesh['grp'=16,'tp'=8] {'grp','tp'}, dimensions={0} | all-to-all | bytes 16777216 | tf_op jit(solution)/shard_map/all_to_all | solution.py:279
  114.7 0.0 copy-done
  114.7 7.3 %grow.1 = bf16[128,128,256]{2,1,0:T(8,128)(2,1)} custom-call(s32[8,128]{1,0:T(8,128)} %copy-done, bf16[2,256,256]{2,1,0:T(8,128)(2,1)} %bitcast.4, bf16[128,128,256]{2,1,0:T(8,128)(2,1)} %all_to_all.10.recv_ref), custom_call_target="tpu_custom_call" | custom-call | tf_op jit(solution)/shard_map/grow/pallas_call | solution.py:283
  122.0 8.0 %all-to-all-start.1 = ((bf16[128,128,256]{2,1,0:T(8,128)(2,1)}), bf16[128,128,256]{2,1,0:T(8,128)(2,1)}, u32[]{:S(2)}, u32[]{:S(2)}) async-start(bf16[128,128,256]{2,1,0:T(8,128)(2,1)} %grow.1), calls=%async_computation.1 | async-start | bytes 16777216 | tf_op jit(solution)/shard_map/all_to_all | solution.py:298
  130.0 35.7 %attend.1 = bf16[2,8,256,128]{3,2,1,0:T(8,128)(2,1)} custom-call(s32[8,128]{1,0:T(8,128)} %copy-done, bf16[2,8,256,128]{3,2,1,0:T(8,128)(2,1)} %queries_ref.1, bf16[2,256,256]{2,1,0:T(8,128)(2,1)} %bitcast.5, bf16[128,128,256]{2,1,0:T(8,128)(2,1)} %all_to_all.10.recv_ref), custom_call_target="tpu_custom_call" | custom-call | flops 17179869184 | bytes 8388608 | tf_op jit(solution)/shard_map/attend/pallas_call | solution.py:300
  165.7 66.9 %all-to-all-done.1 = bf16[128,128,256]{2,1,0:T(8,128)(2,1)} async-done(((bf16[128,128,256]{2,1,0:T(8,128)(2,1)}), bf16[128,128,256]{2,1,0:T(8,128)(2,1)}, u32[]{:S(2)}, u32[]{:S(2)}) %all-to-all-start.1) | async-done | bytes 8388640 | tf_op jit(solution)/shard_map/all_to_all | solution.py:298
  232.6 6.2 %unpack.1 = bf16[16,8,128,256]{3,2,1,0:T(8,128)(2,1)} custom-call(s32[8,128]{1,0:T(8,128)} %copy-done, bf16[16,8,128,256]{3,2,1,0:T(8,128)(2,1)} %bitcast.2.arrived_ref), custom_call_target="tpu_custom_call" | custom-call | tf_op jit(solution)/shard_map/unpack/pallas_call | solution.py:320
Async XLA Ops:
  4.7 110.0 %copy-start = (s32[8,128]{1,0:T(8,128)}, s32[8,128]{1,0:T(8,128)S(1)}, u32[]{:S(2)}) copy-start(s32[8,128]{1,0:T(8,128)S(1)} %get-tuple-element.4.table_ref) | copy-start | bytes 12292
  122.0 110.6 %all-to-all-start.1 = ((bf16[128,128,256]{2,1,0:T(8,128)(2,1)}), bf16[128,128,256]{2,1,0:T(8,128)(2,1)}, u32[]{:S(2)}, u32[]{:S(2)}) async-start(bf16[128,128,256]{2,1,0:T(8,128)(2,1)} %grow.1), calls=%async_computation.1 | async-start | bytes 16777216 | tf_op jit(solution)/shard_map/all_to_all | solution.py:298

commit v4 on v3

--- a/solution.py
+++ b/solution.py
@@ -10,35 +10,40 @@
 
 MASKED = -1e30
 CHUNK_BLOCKS = 8
-PICK, TARGET, LENGTHS, EDGES, CODES, SOURCES = range(6)
+PICK, TARGET, LENGTHS, EDGES, CODES, BLOCKS = range(6)
 TABLE_ROWS = 8
 VMEM_LIMIT = 60 * 1024 * 1024
-PACK_LIMIT = 40 * 1024 * 1024
+PACK_LIMIT = 24 * 1024 * 1024
+GROW_LIMIT = 24 * 1024 * 1024
+ATTEND_LIMIT = 60 * 1024 * 1024
 
 
 def pack_kernel(
-    packed_ref, pool_ref, out_ref, table_ref, sems, *, seats, turn
+    seat_ref, lens_ref, old_ref, new_ref, pool_ref, out_ref, table_ref, sems, *, seats, turn
 ):
     count, tp_count, block_len = pool_ref.shape[:3]
-    sessions, max_blocks = packed_ref.shape[0], packed_ref.shape[1] // 2
+    sessions, max_blocks = old_ref.shape
     owners = table_ref.shape[1]
     spill = turn // block_len + 1
     my_group = lax.axis_index("grp")
     first_slot = (my_group * tp_count + lax.axis_index("tp")) * count
 
     shape = (sessions, max_blocks)
+    session = lax.broadcasted_iota(jnp.int32, shape, 0)
     block = lax.broadcasted_iota(jnp.int32, shape, 1)
-    slots = owners * count
-    old = lax.rem(packed_ref[:, :max_blocks], slots)
-    new = lax.div(packed_ref[:, :max_blocks], slots)
-    length = lax.div(packed_ref[:, max_blocks:], sessions)
-    seat = lax.rem(packed_ref[:, max_blocks:], sessions)
+    seat = jnp.zeros(shape, jnp.int32)
+    length = jnp.zeros(shape, jnp.int32)
+    for s in range(sessions):
+        seat = jnp.where(session == s, seat_ref[s], seat)
+        length = jnp.where(session == s, lens_ref[s], length)
     group = lax.div(seat, seats)
 
     def codes_of(slots, lengths):
         code = jnp.where(block * block_len < lengths, group + 1, 0)
         return [jnp.sum(jnp.where(slots - first_slot == i, code, 0)) for i in range(count)]
 
+    old = old_ref[...]
+    new = new_ref[...]
     codes = codes_of(old, length)
 
     def copy(i):
@@ -78,12 +83,12 @@
         pick = jnp.where(on_edge, owners + q * spill + past, source)
         from_owner = owner == column(source)
         pick_row += jnp.sum(jnp.where(from_owner, column(pick), 0), axis=0, keepdims=True)
-        target = column(of_seat(lax.div(new, count)))
-        target_row += jnp.sum(jnp.where(from_owner, target, 0), axis=0, keepdims=True)
+        target = of_seat(lax.div(new, count))
+        target_row += jnp.sum(jnp.where(from_owner, column(target), 0), axis=0, keepdims=True)
         edge = jnp.sum(jnp.where(past == 0, source, 0), axis=1, keepdims=True)
         edge_row = jnp.where(lane == q, edge, edge_row)
         length_row = jnp.where(lane == q, my_length[:, :1], length_row)
-        table_ref[SOURCES + q : SOURCES + q + 1, :max_blocks] = source
+        table_ref[BLOCKS + q : BLOCKS + q + 1, :max_blocks] = target
     table_ref[PICK : PICK + 1, :] = pick_row
     table_ref[TARGET : TARGET + 1, :] = target_row
     table_ref[LENGTHS : LENGTHS + 1, :] = length_row
@@ -118,26 +123,23 @@
 
 
 def grow_kernel(
-    table_ref, fresh_ref, recv_ref, out_ref,
-    held, edge_in, load_sems, store_sem, edge_sems,
+    table_ref, fresh_ref, recv_ref, out_ref, grown, edge_in, store_sem, edge_sems
 ):
     owners, block_len, width = recv_ref.shape
     seats, turn = fresh_ref.shape[:2]
     spill = turn // block_len + 1
-    parts = load_sems.shape[0]
-    share = owners // parts
-
-    def load(c):
-        rows = pl.ds(c * share, share)
-        return pltpu.make_async_copy(recv_ref.at[rows], held.at[rows], load_sems.at[c])
 
     def edge_load(q):
-        return pltpu.make_async_copy(recv_ref.at[table_ref[EDGES, q]], edge_in.at[q], edge_sems.at[q])
+        row = recv_ref.at[table_ref[EDGES, q]]
+        return pltpu.make_async_copy(row, edge_in.at[q], edge_sems.at[q])
+
+    def send(o, source):
+        pltpu.make_async_copy(source, out_ref.at[table_ref[TARGET, o]], store_sem).start()
 
     for q in range(seats):
         edge_load(q).start()
-    for c in range(parts):
-        load(c).start()
+    for o in range(owners):
+        pl.when(table_ref[PICK, o] < owners)(lambda o=o: send(o, recv_ref.at[o]))
     row = lax.broadcasted_iota(jnp.int32, (block_len, width), 0)
     for q in range(seats):
         rest = lax.rem(table_ref[LENGTHS, q], block_len)
@@ -146,23 +148,24 @@
         moved = pltpu.roll(moved, rest, 0)
         edge_load(q).wait()
         first = jnp.where(row < rest, edge_in[q].astype(jnp.float32), moved[:block_len])
-        held[owners + q * spill] = first.astype(held.dtype)
+        grown[q * spill] = first.astype(grown.dtype)
         for k in range(1, spill):
             later = moved[k * block_len : (k + 1) * block_len]
-            held[owners + q * spill + k] = later.astype(held.dtype)
-    for c in range(parts):
-        load(c).wait()
-        for o in range(c * share, (c + 1) * share):
-            row_in, row_out = held.at[table_ref[PICK, o]], out_ref.at[table_ref[TARGET, o]]
-            pltpu.make_async_copy(row_in, row_out, store_sem).start()
-    pltpu.make_async_copy(held.at[pl.ds(0, owners)], out_ref, store_sem).wait()
+            grown[q * spill + k] = later.astype(grown.dtype)
+
+    @pl.loop(0, owners)
+    def _(o):
+        pick = table_ref[PICK, o]
+        pl.when(pick >= owners)(lambda: send(o, grown.at[pick - owners]))
+
+    pltpu.make_async_copy(recv_ref, out_ref, store_sem).wait()
 
 
 def attend_kernel(
-    table_ref, queries_ref, fresh_ref, recv_ref, out_ref, cache, acc, high, sems
+    table_ref, queries_ref, fresh_ref, grown_ref, out_ref, cache, acc, high, sems
 ):
     seats = queries_ref.shape[0]
-    block_len = recv_ref.shape[1]
+    block_len = grown_ref.shape[1]
     head_dim = queries_ref.shape[3]
     heads = queries_ref.shape[1]
     turn = queries_ref.shape[2]
@@ -172,7 +175,7 @@
 
     def row_copy(q, j):
         return pltpu.make_async_copy(
-            recv_ref.at[table_ref[SOURCES + q, j]],
+            grown_ref.at[table_ref[BLOCKS + q, j]],
             cache.at[q, pl.ds(pl.multiple_of(j * block_len, block_len), block_len)],
             sems.at[q, j],
         )
@@ -254,6 +257,7 @@
     owners = group_count * tp_count
     assert pool_dev == group_count and kv_heads == tp_count and max_blocks <= owners
     dtype = kv_pool.dtype
+    in_hbm = functools.partial(pltpu.with_memory_space_constraint, memory_space=pltpu.HBM)
     anywhere = pl.BlockSpec(memory_space=pl.ANY)
     vmem = pl.BlockSpec(memory_space=pltpu.VMEM)
     smem = pl.BlockSpec(memory_space=pltpu.SMEM)
@@ -262,20 +266,15 @@
     fresh = new_kv.reshape(seats_group, turn, pair_width)
     spill = turn // block_len + 1
 
-    session = cache_lens * session_seat.shape[0] + session_seat
-    packed = jnp.concatenate(
-        [new_slots * (owners * pool_dev) + old_slots, jnp.broadcast_to(session[:, None], old_slots.shape)],
-        axis=1,
-    )
     outgoing, table = pl.pallas_call(
         functools.partial(pack_kernel, seats=seats_group, turn=turn),
-        in_specs=[vmem, anywhere],
+        in_specs=[smem, smem, vmem, vmem, anywhere],
         out_specs=[anywhere, vmem],
         scratch_shapes=[pltpu.SemaphoreType.DMA((group_count,))],
-        out_shape=[blocks, jax.ShapeDtypeStruct((TABLE_ROWS, owners), jnp.int32)],
+        out_shape=[pltpu.VMEM(blocks.shape, dtype), pltpu.HBM((TABLE_ROWS, owners), jnp.int32)],
         compiler_params=pltpu.CompilerParams(vmem_limit_bytes=PACK_LIMIT),
         name="pack",
-    )(packed, kv_pool)
+    )(*map(in_hbm, (session_seat, cache_lens, old_slots, new_slots, kv_pool)))
     received = lax.all_to_all(
         outgoing.reshape(rows.shape), ("grp", "tp"), split_axis=0, concat_axis=0, tiled=True
     )
@@ -285,16 +284,15 @@
         in_specs=[smem, vmem, anywhere],
         out_specs=anywhere,
         scratch_shapes=[
-            pltpu.VMEM((owners + seats_group * spill, block_len, pair_width), dtype),
+            pltpu.VMEM((seats_group * spill, block_len, pair_width), dtype),
             pltpu.VMEM((seats_group, block_len, pair_width), dtype),
-            pltpu.SemaphoreType.DMA((8,)),
             pltpu.SemaphoreType.DMA,
             pltpu.SemaphoreType.DMA((seats_group,)),
         ],
-        out_shape=rows,
-        compiler_params=pltpu.CompilerParams(vmem_limit_bytes=VMEM_LIMIT),
+        out_shape=pltpu.HBM(rows.shape, dtype),
+        compiler_params=pltpu.CompilerParams(vmem_limit_bytes=GROW_LIMIT),
         name="grow",
-    )(table, fresh, received)
+    )(table, fresh, pltpu.with_memory_space_constraint(received, pltpu.VMEM))
     arrived = lax.all_to_all(leaving, ("grp", "tp"), split_axis=0, concat_axis=0, tiled=True)
 
     attention = pl.pallas_call(
@@ -308,14 +306,14 @@
             pltpu.SemaphoreType.DMA((seats_group, max_blocks)),
         ],
         out_shape=jax.ShapeDtypeStruct(queries.shape, dtype),
-        compiler_params=pltpu.CompilerParams(vmem_limit_bytes=VMEM_LIMIT),
+        compiler_params=pltpu.CompilerParams(vmem_limit_bytes=ATTEND_LIMIT),
         cost_estimate=pl.CostEstimate(
             flops=4 * seats_group * heads * turn * max_blocks * block_len * head_dim,
             bytes_accessed=owners * block_len * pair_width * 2,
             transcendentals=seats_group * heads * turn * max_blocks * block_len,
         ),
         name="attend",
-    )(table, queries, fresh, received)
+    )(table, in_hbm(queries), fresh, in_hbm(leaving))
 
     new_pool = pl.pallas_call(
         unpack_kernel,

time: 241 us -> 238 us (0.988)
  waiting for transfers between devices: 66.9 us -> 45.4 us
  Pallas kernels: 51.7 us -> 71.4 us
    all_to_all x1, waiting for transfers between devices: 66.9 us -> 45.4 us  [local(): lax.all_to_all(leaving, ('grp', 'tp'), split_axis=0, concat_axis=0, tiled...]
    pallas_call x1, Pallas kernels: 35.7 us -> 57.2 us  [local(): pl.pallas_call(attend_kernel, in_specs=[smem, vmem, vmem, anywhere], out_...]
    pallas_call x1, Pallas kernels: 7.31 us -> 4.01 us  [local(): pl.pallas_call(grow_kernel, in_specs=[smem, vmem, anywhere], out_specs=an...]
  transfers between devices with their start and end apart: 1 -> 1, of which waited for: 1 -> 1; matrix products, arithmetic and copies ran while one was open for 0% -> 0% of each run, Pallas kernels for 15% -> 24%
where the time goes in v4:
time: 238 us; the launch traced here: 235 us
  blocking collectives  110 us (46%)
  Pallas kernels  71.4 us (30%)
  waiting for transfers between devices  45.4 us (19%)
  starting transfers between devices  8.25 us (3%)
    all_to_all x1, blocking collectives, local(): lax.all_to_all(outgoing.reshape(rows.shape), ('grp', 'tp'), split_axis=0,...  110 us
    pallas_call x1, Pallas kernels, local(): pl.pallas_call(attend_kernel, in_specs=[smem, vmem, vmem, anywhere], out_...  57.2 us
    all_to_all x1, waiting for transfers between devices, local(): lax.all_to_all(leaving, ('grp', 'tp'), split_axis=0, concat_axis=0, tiled...  45.4 us
    all_to_all x1, starting transfers between devices, local(): lax.all_to_all(leaving, ('grp', 'tp'), split_axis=0, concat_axis=0, tiled...  8.25 us
    pallas_call x1, Pallas kernels, local(): pl.pallas_call(unpack_kernel, in_specs=[smem, anywhere], out_specs=anywhe...  6.17 us
  transfers between devices with their start and end apart: 1, of which 1 were waited for; matrix products, arithmetic and copies ran while one was open for 0% of the time, Pallas kernels for 24%

profile of v4, /device:TPU:1, one launch (start us, length us, event | category | flops | bytes accessed | tf_op | source)
XLA Modules:
  0.0 235.3 jit_solution(4532404972048332444)
XLA Ops:
  0.6 4.0 %pack.1 = (bf16[16,8,128,256]{3,2,1,0:T(8,128)(2,1)S(1)}, s32[8,128]{1,0:T(8,128)}) custom-call(s32[32]{0:T(128)} %seat_ref.1, s32[32]{0:T(128)} %lens_ref.1, s32[32,64]{1,0:T(8,128)} %old_ref.1, s32[32,64]{1,0:T(8,128)} %new_ref.1, bf16[16,8,128,256]{3,2,1,0:T(8,128)(2,1)} %pool_ref.1), custom_call_target="tpu_custom_call" | custom-call | tf_op jit(solution)/shard_map/pack/pallas_call | solution.py:269
  4.6 0.0 copy-start
  4.6 0.0 copy-start.1
  4.6 109.6 %all_to_all.10.recv_ref = bf16[128,128,256]{2,1,0:T(8,128)(2,1)S(1)} all-to-all(bf16[128,128,256]{2,1,0:T(8,128)(2,1)S(1)} %bitcast.3), channel_id=1, replica_groups=mesh['grp'=16,'tp'=8] {'grp','tp'}, dimensions={0} | all-to-all | bytes 16777216 | tf_op jit(solution)/shard_map/all_to_all | solution.py:278
  114.2 0.0 copy-done
  114.2 0.0 copy-done.1
  114.2 4.0 %grow.1.grown_ref = bf16[128,128,256]{2,1,0:T(8,128)(2,1)} custom-call(s32[8,128]{1,0:T(8,128)S(1)} %copy-done.1, bf16[2,256,256]{2,1,0:T(8,128)(2,1)S(1)} %bitcast.5, bf16[128,128,256]{2,1,0:T(8,128)(2,1)S(1)} %all_to_all.10.recv_ref), custom_call_target="tpu_custom_call" | custom-call | tf_op jit(solution)/shard_map/grow/pallas_call | solution.py:282
  118.2 8.2 %all-to-all-start.1 = ((bf16[128,128,256]{2,1,0:T(8,128)(2,1)}), bf16[128,128,256]{2,1,0:T(8,128)(2,1)}, u32[]{:S(2)}, u32[]{:S(2)}) async-start(bf16[128,128,256]{2,1,0:T(8,128)(2,1)} %grow.1.grown_ref), calls=%async_computation.1 | async-start | bytes 16777216 | tf_op jit(solution)/shard_map/all_to_all | solution.py:296
  126.5 57.2 %attend.1 = bf16[2,8,256,128]{3,2,1,0:T(8,128)(2,1)} custom-call(s32[8,128]{1,0:T(8,128)} %get-tuple-element.4.table_ref, bf16[2,8,256,128]{3,2,1,0:T(8,128)(2,1)} %queries_ref.1, bf16[2,256,256]{2,1,0:T(8,128)(2,1)} %bitcast.4, bf16[128,128,256]{2,1,0:T(8,128)(2,1)} %grow.1.grown_ref), custom_call_target="tpu_custom_call" | custom-call | flops 17179869184 | bytes 8388608 | tf_op jit(solution)/shard_map/attend/pallas_call | solution.py:298
  183.7 45.4 %all-to-all-done.1 = bf16[128,128,256]{2,1,0:T(8,128)(2,1)} async-done(((bf16[128,128,256]{2,1,0:T(8,128)(2,1)}), bf16[128,128,256]{2,1,0:T(8,128)(2,1)}, u32[]{:S(2)}, u32[]{:S(2)}) %all-to-all-start.1) | async-done | bytes 8388640 | tf_op jit(solution)/shard_map/all_to_all | solution.py:296
  229.1 6.2 %unpack.1 = bf16[16,8,128,256]{3,2,1,0:T(8,128)(2,1)} custom-call(s32[8,128]{1,0:T(8,128)} %get-tuple-element.4.table_ref, bf16[16,8,128,256]{3,2,1,0:T(8,128)(2,1)} %bitcast.2.arrived_ref), custom_call_target="tpu_custom_call" | custom-call | tf_op jit(solution)/shard_map/unpack/pallas_call | solution.py:318
Async XLA Ops:
  4.6 109.6 %copy-start = (bf16[2,1,256,256]{3,2,1,0:T(8,128)(2,1)S(1)}, bf16[2,1,256,256]{3,2,1,0:T(8,128)(2,1)}, u32[]{:S(2)}) copy-start(bf16[2,1,256,256]{3,2,1,0:T(8,128)(2,1)} %param.8) | copy-start | bytes 786436
  4.6 109.6 %copy-start.1 = (s32[8,128]{1,0:T(8,128)S(1)}, s32[8,128]{1,0:T(8,128)}, u32[]{:S(2)}) copy-start(s32[8,128]{1,0:T(8,128)} %get-tuple-element.4.table_ref) | copy-start | bytes 12292
  118.2 110.9 %all-to-all-start.1 = ((bf16[128,128,256]{2,1,0:T(8,128)(2,1)}), bf16[128,128,256]{2,1,0:T(8,128)(2,1)}, u32[]{:S(2)}, u32[]{:S(2)}) async-start(bf16[128,128,256]{2,1,0:T(8,128)(2,1)} %grow.1.grown_ref), calls=%async_computation.1 | async-start | bytes 16777216 | tf_op jit(solution)/shard_map/all_to_all | solution.py:296

commit v5 on v4

--- a/solution.py
+++ b/solution.py
@@ -22,6 +22,7 @@
     seat_ref, lens_ref, old_ref, new_ref, pool_ref, out_ref, table_ref, sems, *, seats, turn
 ):
     count, tp_count, block_len = pool_ref.shape[:3]
+    groups = out_ref.shape[1]
     sessions, max_blocks = old_ref.shape
     owners = table_ref.shape[1]
     spill = turn // block_len + 1
@@ -44,10 +45,15 @@
 
     old = old_ref[...]
     new = new_ref[...]
+
+    def rank_of(slots):
+        device = lax.div(slots, count)
+        return lax.rem(device, tp_count) * groups + lax.div(device, tp_count)
+
     codes = codes_of(old, length)
 
     def copy(i):
-        return pltpu.make_async_copy(pool_ref.at[i], out_ref.at[codes[i] - 1], sems.at[i])
+        return pltpu.make_async_copy(pool_ref.at[i], out_ref.at[:, codes[i] - 1], sems.at[i])
 
     for i in range(count):
         pl.when(codes[i] > 0)(lambda i=i: copy(i).start())
@@ -77,13 +83,13 @@
             return jnp.sum(jnp.where(diagonal, row, 0), axis=1, keepdims=True)
 
         my_length = of_seat(length)
-        source = of_seat(lax.div(old, count))
+        source = of_seat(rank_of(old))
         past = place - lax.div(my_length, block_len)
         on_edge = jnp.logical_and(past >= 0, past < spill)
         pick = jnp.where(on_edge, owners + q * spill + past, source)
         from_owner = owner == column(source)
         pick_row += jnp.sum(jnp.where(from_owner, column(pick), 0), axis=0, keepdims=True)
-        target = of_seat(lax.div(new, count))
+        target = of_seat(rank_of(new))
         target_row += jnp.sum(jnp.where(from_owner, column(target), 0), axis=0, keepdims=True)
         edge = jnp.sum(jnp.where(past == 0, source, 0), axis=1, keepdims=True)
         edge_row = jnp.where(lane == q, edge, edge_row)
@@ -101,7 +107,7 @@
     count = out_ref.shape[0]
 
     def load(i):
-        source = arrived_ref.at[table_ref[CODES, i] - 1]
+        source = arrived_ref.at[:, table_ref[CODES, i] - 1]
         return pltpu.make_async_copy(source, held.at[i], load_sems.at[i])
 
     def store(i, source):
@@ -263,6 +269,7 @@
     smem = pl.BlockSpec(memory_space=pltpu.SMEM)
     rows = jax.ShapeDtypeStruct((owners, block_len, pair_width), dtype)
     blocks = jax.ShapeDtypeStruct((group_count, kv_heads, block_len, pair_width), dtype)
+    by_head = jax.ShapeDtypeStruct((kv_heads, group_count, block_len, pair_width), dtype)
     fresh = new_kv.reshape(seats_group, turn, pair_width)
     spill = turn // block_len + 1
 
@@ -271,12 +278,12 @@
         in_specs=[smem, smem, vmem, vmem, anywhere],
         out_specs=[anywhere, vmem],
         scratch_shapes=[pltpu.SemaphoreType.DMA((group_count,))],
-        out_shape=[pltpu.VMEM(blocks.shape, dtype), pltpu.HBM((TABLE_ROWS, owners), jnp.int32)],
+        out_shape=[pltpu.VMEM(by_head.shape, dtype), pltpu.HBM((TABLE_ROWS, owners), jnp.int32)],
         compiler_params=pltpu.CompilerParams(vmem_limit_bytes=PACK_LIMIT),
         name="pack",
     )(*map(in_hbm, (session_seat, cache_lens, old_slots, new_slots, kv_pool)))
     received = lax.all_to_all(
-        outgoing.reshape(rows.shape), ("grp", "tp"), split_axis=0, concat_axis=0, tiled=True
+        outgoing.reshape(rows.shape), ("tp", "grp"), split_axis=0, concat_axis=0, tiled=True
     )
 
     leaving = pl.pallas_call(
@@ -293,7 +300,7 @@
         compiler_params=pltpu.CompilerParams(vmem_limit_bytes=GROW_LIMIT),
         name="grow",
     )(table, fresh, pltpu.with_memory_space_constraint(received, pltpu.VMEM))
-    arrived = lax.all_to_all(leaving, ("grp", "tp"), split_axis=0, concat_axis=0, tiled=True)
+    arrived = lax.all_to_all(leaving, ("tp", "grp"), split_axis=0, concat_axis=0, tiled=True)
 
     attention = pl.pallas_call(
         attend_kernel,
@@ -328,7 +335,7 @@
         out_shape=blocks,
         compiler_params=pltpu.CompilerParams(vmem_limit_bytes=VMEM_LIMIT),
         name="unpack",
-    )(table, arrived.reshape(blocks.shape))
+    )(table, arrived.reshape(by_head.shape))
     return attention, new_pool
 
 

time: 238 us -> 230 us (0.966)
  waiting for transfers between devices: 45.4 us -> 39.2 us
  Pallas kernels: 71.4 us -> 75.8 us
  starting transfers between devices: 8.25 us -> 4.88 us
    all_to_all x1, waiting for transfers between devices: 45.4 us -> 39.2 us  [local(): lax.all_to_all(leaving, ('tp', 'grp'), split_axis=0, concat_axis=0, tiled...]
    pallas_call x1, Pallas kernels: 57.2 us -> 61.6 us  [local(): pl.pallas_call(attend_kernel, in_specs=[smem, vmem, vmem, anywhere], out_...]
    all_to_all x1, starting transfers between devices: 8.25 us -> 4.88 us  [local(): lax.all_to_all(leaving, ('tp', 'grp'), split_axis=0, concat_axis=0, tiled...]
  transfers between devices with their start and end apart: 1 -> 1, of which waited for: 1 -> 1; matrix products, arithmetic and copies ran while one was open for 0% -> 0% of each run, Pallas kernels for 24% -> 27%
where the time goes in v5:
time: 230 us
  blocking collectives  109 us (47%)
  Pallas kernels  75.8 us (33%)
  waiting for transfers between devices  39.2 us (17%)
  starting transfers between devices  4.88 us (2%)
    all_to_all x1, blocking collectives, local(): lax.all_to_all(outgoing.reshape(rows.shape), ('tp', 'grp'), split_axis=0,...  109 us
    pallas_call x1, Pallas kernels, local(): pl.pallas_call(attend_kernel, in_specs=[smem, vmem, vmem, anywhere], out_...  61.6 us
    all_to_all x1, waiting for transfers between devices, local(): lax.all_to_all(leaving, ('tp', 'grp'), split_axis=0, concat_axis=0, tiled...  39.2 us
    pallas_call x1, Pallas kernels, local(): pl.pallas_call(unpack_kernel, in_specs=[smem, anywhere], out_specs=anywhe...  6.16 us
    all_to_all x1, starting transfers between devices, local(): lax.all_to_all(leaving, ('tp', 'grp'), split_axis=0, concat_axis=0, tiled...  4.88 us
  transfers between devices with their start and end apart: 1, of which 1 were waited for; matrix products, arithmetic and copies ran while one was open for 0% of the time, Pallas kernels for 27%

profile of v5, /device:TPU:1, one launch (start us, length us, event | category | flops | bytes accessed | tf_op | source)
XLA Modules:
  0.0 229.5 jit_solution(11535527722712607222)
XLA Ops:
  0.6 4.0 %pack.1 = (bf16[8,16,128,256]{3,2,1,0:T(8,128)(2,1)S(1)}, s32[8,128]{1,0:T(8,128)}) custom-call(s32[32]{0:T(128)} %seat_ref.1, s32[32]{0:T(128)} %lens_ref.1, s32[32,64]{1,0:T(8,128)} %old_ref.1, s32[32,64]{1,0:T(8,128)} %new_ref.1, bf16[16,8,128,256]{3,2,1,0:T(8,128)(2,1)} %pool_ref.1), custom_call_target="tpu_custom_call" | custom-call | tf_op jit(solution)/shard_map/pack/pallas_call | solution.py:276
  4.6 0.0 copy-start
  4.6 0.0 copy-start.1
  4.6 109.0 %all_to_all.10.recv_ref = bf16[128,128,256]{2,1,0:T(8,128)(2,1)S(1)} all-to-all(bf16[128,128,256]{2,1,0:T(8,128)(2,1)S(1)} %bitcast.3), channel_id=1, replica_groups=mesh['grp'=16,'tp'=8] {'tp','grp'}, dimensions={0} | all-to-all | bytes 16777216 | tf_op jit(solution)/shard_map/all_to_all | solution.py:285
  113.6 0.0 copy-done
  113.6 0.0 copy-done.1
  113.6 4.0 %grow.1.grown_ref = bf16[128,128,256]{2,1,0:T(8,128)(2,1)} custom-call(s32[8,128]{1,0:T(8,128)S(1)} %copy-done.1, bf16[2,256,256]{2,1,0:T(8,128)(2,1)S(1)} %bitcast.5, bf16[128,128,256]{2,1,0:T(8,128)(2,1)S(1)} %all_to_all.10.recv_ref), custom_call_target="tpu_custom_call" | custom-call | tf_op jit(solution)/shard_map/grow/pallas_call | solution.py:289
  117.7 4.9 %all-to-all-start.1 = ((bf16[128,128,256]{2,1,0:T(8,128)(2,1)}), bf16[128,128,256]{2,1,0:T(8,128)(2,1)}, u32[]{:S(2)}, u32[]{:S(2)}) async-start(bf16[128,128,256]{2,1,0:T(8,128)(2,1)} %grow.1.grown_ref), calls=%async_computation.1 | async-start | bytes 16777216 | tf_op jit(solution)/shard_map/all_to_all | solution.py:303
  122.5 61.6 %attend.1 = bf16[2,8,256,128]{3,2,1,0:T(8,128)(2,1)} custom-call(s32[8,128]{1,0:T(8,128)} %get-tuple-element.4.table_ref, bf16[2,8,256,128]{3,2,1,0:T(8,128)(2,1)} %queries_ref.1, bf16[2,256,256]{2,1,0:T(8,128)(2,1)} %bitcast.4, bf16[128,128,256]{2,1,0:T(8,128)(2,1)} %grow.1.grown_ref), custom_call_target="tpu_custom_call" | custom-call | flops 17179869184 | bytes 8388608 | tf_op jit(solution)/shard_map/attend/pallas_call | solution.py:305
  184.2 39.2 %all-to-all-done.1 = bf16[128,128,256]{2,1,0:T(8,128)(2,1)} async-done(((bf16[128,128,256]{2,1,0:T(8,128)(2,1)}), bf16[128,128,256]{2,1,0:T(8,128)(2,1)}, u32[]{:S(2)}, u32[]{:S(2)}) %all-to-all-start.1) | async-done | bytes 8388640 | tf_op jit(solution)/shard_map/all_to_all | solution.py:303
  223.4 6.2 %unpack.1 = bf16[16,8,128,256]{3,2,1,0:T(8,128)(2,1)} custom-call(s32[8,128]{1,0:T(8,128)} %get-tuple-element.4.table_ref, bf16[8,16,128,256]{3,2,1,0:T(8,128)(2,1)} %bitcast.2.arrived_ref), custom_call_target="tpu_custom_call" | custom-call | tf_op jit(solution)/shard_map/unpack/pallas_call | solution.py:325
Async XLA Ops:
  4.6 109.0 %copy-start = (bf16[2,1,256,256]{3,2,1,0:T(8,128)(2,1)S(1)}, bf16[2,1,256,256]{3,2,1,0:T(8,128)(2,1)}, u32[]{:S(2)}) copy-start(bf16[2,1,256,256]{3,2,1,0:T(8,128)(2,1)} %param.8) | copy-start | bytes 786436
  4.6 109.0 %copy-start.1 = (s32[8,128]{1,0:T(8,128)S(1)}, s32[8,128]{1,0:T(8,128)}, u32[]{:S(2)}) copy-start(s32[8,128]{1,0:T(8,128)} %get-tuple-element.4.table_ref) | copy-start | bytes 12292
  117.7 105.7 %all-to-all-start.1 = ((bf16[128,128,256]{2,1,0:T(8,128)(2,1)}), bf16[128,128,256]{2,1,0:T(8,128)(2,1)}, u32[]{:S(2)}, u32[]{:S(2)}) async-start(bf16[128,128,256]{2,1,0:T(8,128)(2,1)} %grow.1.grown_ref), calls=%async_computation.1 | async-start | bytes 16777216 | tf_op jit(solution)/shard_map/all_to_all | solution.py:303

commit v6 on v5

--- a/solution.py
+++ b/solution.py
@@ -103,29 +103,26 @@
         pl.when(codes[i] > 0)(lambda i=i: copy(i).wait())
 
 
-def unpack_kernel(table_ref, arrived_ref, out_ref, held, zeros, load_sems, store_sems):
+def unpack_kernel(table_ref, arrived_ref, cleared_ref, out_ref, held, load_sems, store_sems):
     count = out_ref.shape[0]
 
     def load(i):
         source = arrived_ref.at[:, table_ref[CODES, i] - 1]
         return pltpu.make_async_copy(source, held.at[i], load_sems.at[i])
 
-    def store(i, source):
-        return pltpu.make_async_copy(source, out_ref.at[i], store_sems.at[i])
+    def store(i):
+        return pltpu.make_async_copy(held.at[i], out_ref.at[i], store_sems.at[i])
 
     def forward(i):
         load(i).wait()
-        store(i, held.at[i]).start()
+        store(i).start()
 
     for i in range(count):
         pl.when(table_ref[CODES, i] > 0)(lambda i=i: load(i).start())
-    zeros[...] = jnp.zeros_like(zeros)
-    for i in range(count):
-        pl.when(table_ref[CODES, i] == 0)(lambda i=i: store(i, zeros).start())
     for i in range(count):
         pl.when(table_ref[CODES, i] > 0)(lambda i=i: forward(i))
     for i in range(count):
-        store(i, zeros).wait()
+        pl.when(table_ref[CODES, i] > 0)(lambda i=i: store(i).wait())
 
 
 def grow_kernel(
@@ -168,7 +165,8 @@
 
 
 def attend_kernel(
-    table_ref, queries_ref, fresh_ref, grown_ref, out_ref, cache, acc, high, sems
+    table_ref, queries_ref, fresh_ref, grown_ref, out_ref, cleared_ref,
+    cache, acc, high, zeros, sems, clear_sems,
 ):
     seats = queries_ref.shape[0]
     block_len = grown_ref.shape[1]
@@ -186,6 +184,9 @@
             sems.at[q, j],
         )
 
+    def clear(i):
+        return pltpu.make_async_copy(zeros, cleared_ref.at[i], clear_sems.at[i])
+
     def blocks_of(q):
         return (table_ref[LENGTHS, q] + block_len - 1) // block_len
 
@@ -194,6 +195,11 @@
 
     for q in range(seats):
         pl.loop(0, blocks_of(q))(lambda j, q=q: row_copy(q, j).start())
+
+    slots = cleared_ref.shape[0]
+    zeros[...] = jnp.zeros_like(zeros)
+    for i in range(slots):
+        pl.when(table_ref[CODES, i] == 0)(lambda i=i: clear(i).start())
 
     def values_of(rows):
         ones = jnp.ones((rows.shape[0], head_dim), rows.dtype)
@@ -252,6 +258,9 @@
             for k in range(pair):
                 total = acc[k, :, head_dim : head_dim + 1]
                 out_ref[q, h * pair + k] = (acc[k, :, :head_dim] / total).astype(out_ref.dtype)
+
+    for i in range(slots):
+        pl.when(table_ref[CODES, i] == 0)(lambda i=i: clear(i).wait())
 
 
 def local(queries, new_kv, kv_pool, cache_lens, session_seat, old_slots, new_slots):
@@ -302,17 +311,19 @@
     )(table, fresh, pltpu.with_memory_space_constraint(received, pltpu.VMEM))
     arrived = lax.all_to_all(leaving, ("tp", "grp"), split_axis=0, concat_axis=0, tiled=True)
 
-    attention = pl.pallas_call(
+    attention, cleared = pl.pallas_call(
         attend_kernel,
         in_specs=[smem, vmem, vmem, anywhere],
-        out_specs=vmem,
+        out_specs=[vmem, anywhere],
         scratch_shapes=[
             pltpu.VMEM((seats_group, max_blocks * block_len, pair_width), dtype),
             pltpu.VMEM((2, turn, 2 * head_dim), jnp.float32),
             pltpu.VMEM((2, turn, head_dim), jnp.float32),
+            pltpu.VMEM(blocks.shape[1:], dtype),
             pltpu.SemaphoreType.DMA((seats_group, max_blocks)),
+            pltpu.SemaphoreType.DMA((group_count,)),
         ],
-        out_shape=jax.ShapeDtypeStruct(queries.shape, dtype),
+        out_shape=[jax.ShapeDtypeStruct(queries.shape, dtype), pltpu.HBM(blocks.shape, dtype)],
         compiler_params=pltpu.CompilerParams(vmem_limit_bytes=ATTEND_LIMIT),
         cost_estimate=pl.CostEstimate(
             flops=4 * seats_group * heads * turn * max_blocks * block_len * head_dim,
@@ -324,18 +335,18 @@
 
     new_pool = pl.pallas_call(
         unpack_kernel,
-        in_specs=[smem, anywhere],
+        in_specs=[smem, anywhere, anywhere],
         out_specs=anywhere,
         scratch_shapes=[
             pltpu.VMEM(blocks.shape, dtype),
-            pltpu.VMEM(blocks.shape[1:], dtype),
             pltpu.SemaphoreType.DMA((group_count,)),
             pltpu.SemaphoreType.DMA((group_count,)),
         ],
         out_shape=blocks,
         compiler_params=pltpu.CompilerParams(vmem_limit_bytes=VMEM_LIMIT),
+        input_output_aliases={2: 0},
         name="unpack",
-    )(table, arrived.reshape(by_head.shape))
+    )(table, arrived.reshape(by_head.shape), cleared)
     return attention, new_pool
 
 

time: 230 us -> 229 us (level)
  Pallas kernels: 75.8 us -> 54.3 us
  waiting for transfers between devices: 39.2 us -> 59.7 us
    pallas_call x1, Pallas kernels: 61.6 us -> 41.1 us  [local(): pl.pallas_call(attend_kernel, in_specs=[smem, vmem, vmem, anywhere], out_...]
    all_to_all x1, waiting for transfers between devices: 39.2 us -> 59.7 us  [local(): lax.all_to_all(leaving, ('tp', 'grp'), split_axis=0, concat_axis=0, tiled...]
  transfers between devices with their start and end apart: 1 -> 1, of which waited for: 1 -> 1; matrix products, arithmetic and copies ran while one was open for 0% -> 0% of each run, Pallas kernels for 27% -> 18%
where the time goes in v6:
time: 229 us; the launch traced here: 228 us
  blocking collectives  109 us (48%)
  waiting for transfers between devices  59.7 us (26%)
  Pallas kernels  54.3 us (24%)
  starting transfers between devices  4.88 us (2%)
    all_to_all x1, blocking collectives, local(): lax.all_to_all(outgoing.reshape(rows.shape), ('tp', 'grp'), split_axis=0,...  109 us
    all_to_all x1, waiting for transfers between devices, local(): lax.all_to_all(leaving, ('tp', 'grp'), split_axis=0, concat_axis=0, tiled...  59.7 us
    pallas_call x1, Pallas kernels, local(): pl.pallas_call(attend_kernel, in_specs=[smem, vmem, vmem, anywhere], out_...  41.1 us
    pallas_call x1, Pallas kernels, local(): pl.pallas_call(unpack_kernel, in_specs=[smem, anywhere, anywhere], out_sp...  5.01 us
    all_to_all x1, starting transfers between devices, local(): lax.all_to_all(leaving, ('tp', 'grp'), split_axis=0, concat_axis=0, tiled...  4.88 us
  transfers between devices with their start and end apart: 1, of which 1 were waited for; matrix products, arithmetic and copies ran while one was open for 0% of the time, Pallas kernels for 18%

profile of v6, /device:TPU:1, one launch (start us, length us, event | category | flops | bytes accessed | tf_op | source)
XLA Modules:
  0.0 228.5 jit_solution(13612402949629840402)
XLA Ops:
  0.6 4.1 %pack.1 = (bf16[8,16,128,256]{3,2,1,0:T(8,128)(2,1)S(1)}, s32[8,128]{1,0:T(8,128)}) custom-call(s32[32]{0:T(128)} %seat_ref.1, s32[32]{0:T(128)} %lens_ref.1, s32[32,64]{1,0:T(8,128)} %old_ref.1, s32[32,64]{1,0:T(8,128)} %new_ref.1, bf16[16,8,128,256]{3,2,1,0:T(8,128)(2,1)} %pool_ref.1), custom_call_target="tpu_custom_call" | custom-call | tf_op jit(solution)/shard_map/pack/pallas_call | solution.py:285
  4.8 0.0 copy-start
  4.8 0.0 copy-start.1
  4.8 108.9 %all_to_all.10.recv_ref = bf16[128,128,256]{2,1,0:T(8,128)(2,1)S(1)} all-to-all(bf16[128,128,256]{2,1,0:T(8,128)(2,1)S(1)} %bitcast.3), channel_id=1, replica_groups=mesh['grp'=16,'tp'=8] {'tp','grp'}, dimensions={0} | all-to-all | bytes 16777216 | tf_op jit(solution)/shard_map/all_to_all | solution.py:294
  113.7 0.0 copy-done
  113.7 0.0 copy-done.1
  113.7 4.0 %grow.1.grown_ref = bf16[128,128,256]{2,1,0:T(8,128)(2,1)} custom-call(s32[8,128]{1,0:T(8,128)S(1)} %copy-done.1, bf16[2,256,256]{2,1,0:T(8,128)(2,1)S(1)} %bitcast.5, bf16[128,128,256]{2,1,0:T(8,128)(2,1)S(1)} %all_to_all.10.recv_ref), custom_call_target="tpu_custom_call" | custom-call | tf_op jit(solution)/shard_map/grow/pallas_call | solution.py:298
  117.7 4.9 %all-to-all-start.1 = ((bf16[128,128,256]{2,1,0:T(8,128)(2,1)}), bf16[128,128,256]{2,1,0:T(8,128)(2,1)}, u32[]{:S(2)}, u32[]{:S(2)}) async-start(bf16[128,128,256]{2,1,0:T(8,128)(2,1)} %grow.1.grown_ref), calls=%async_computation.1 | async-start | bytes 16777216 | tf_op jit(solution)/shard_map/all_to_all | solution.py:312
  122.6 41.1 %attend.1 = (bf16[2,8,256,128]{3,2,1,0:T(8,128)(2,1)}, bf16[16,8,128,256]{3,2,1,0:T(8,128)(2,1)}) custom-call(s32[8,128]{1,0:T(8,128)} %get-tuple-element.6.table_ref, bf16[2,8,256,128]{3,2,1,0:T(8,128)(2,1)} %queries_ref.1, bf16[2,256,256]{2,1,0:T(8,128)(2,1)} %bitcast.4, bf16[128,128,256]{2,1,0:T(8,128)(2,1)} %grow.1.grown_ref), custom_call_target="tpu_custom_call" | custom-call | flops 17179869184 | bytes 8388608 | tf_op jit(solution)/shard_map/attend/pallas_call | solution.py:314
  163.8 59.7 %all-to-all-done.1 = bf16[128,128,256]{2,1,0:T(8,128)(2,1)} async-done(((bf16[128,128,256]{2,1,0:T(8,128)(2,1)}), bf16[128,128,256]{2,1,0:T(8,128)(2,1)}, u32[]{:S(2)}, u32[]{:S(2)}) %all-to-all-start.1) | async-done | bytes 8388640 | tf_op jit(solution)/shard_map/all_to_all | solution.py:312
  223.5 5.0 %unpack.1 = bf16[16,8,128,256]{3,2,1,0:T(8,128)(2,1)} custom-call(s32[8,128]{1,0:T(8,128)} %get-tuple-element.6.table_ref, bf16[8,16,128,256]{3,2,1,0:T(8,128)(2,1)} %bitcast.2.arrived_ref, bf16[16,8,128,256]{3,2,1,0:T(8,128)(2,1)} %get-tuple-element.9.cleared_ref), custom_call_target="tpu_custom_call", output_to_operand_aliasing={{}: (2, {})} | custom-call | tf_op jit(solution)/shard_map/unpack/pallas_call | solution.py:336
Async XLA Ops:
  4.8 109.0 %copy-start = (bf16[2,1,256,256]{3,2,1,0:T(8,128)(2,1)S(1)}, bf16[2,1,256,256]{3,2,1,0:T(8,128)(2,1)}, u32[]{:S(2)}) copy-start(bf16[2,1,256,256]{3,2,1,0:T(8,128)(2,1)} %param.8) | copy-start | bytes 786436
  4.8 108.9 %copy-start.1 = (s32[8,128]{1,0:T(8,128)S(1)}, s32[8,128]{1,0:T(8,128)}, u32[]{:S(2)}) copy-start(s32[8,128]{1,0:T(8,128)} %get-tuple-element.6.table_ref) | copy-start | bytes 12292
  117.7 105.7 %all-to-all-start.1 = ((bf16[128,128,256]{2,1,0:T(8,128)(2,1)}), bf16[128,128,256]{2,1,0:T(8,128)(2,1)}, u32[]{:S(2)}, u32[]{:S(2)}) async-start(bf16[128,128,256]{2,1,0:T(8,128)(2,1)} %grow.1.grown_ref), calls=%async_computation.1 | async-start | bytes 16777216 | tf_op jit(solution)/shard_map/all_to_all | solution.py:312

commit v7 on v6

--- a/solution.py
+++ b/solution.py
@@ -104,25 +104,27 @@
 
 
 def unpack_kernel(table_ref, arrived_ref, cleared_ref, out_ref, held, load_sems, store_sems):
-    count = out_ref.shape[0]
-
-    def load(i):
-        source = arrived_ref.at[:, table_ref[CODES, i] - 1]
-        return pltpu.make_async_copy(source, held.at[i], load_sems.at[i])
-
-    def store(i):
-        return pltpu.make_async_copy(held.at[i], out_ref.at[i], store_sems.at[i])
-
-    def forward(i):
-        load(i).wait()
-        store(i).start()
-
-    for i in range(count):
-        pl.when(table_ref[CODES, i] > 0)(lambda i=i: load(i).start())
-    for i in range(count):
-        pl.when(table_ref[CODES, i] > 0)(lambda i=i: forward(i))
-    for i in range(count):
-        pl.when(table_ref[CODES, i] > 0)(lambda i=i: store(i).wait())
+    count, parts = load_sems.shape
+    share = held.shape[1] // parts
+    pieces = [(i, pl.ds(k * share, share), k) for k in range(parts) for i in range(count)]
+
+    def load(i, heads, k):
+        source = arrived_ref.at[heads, table_ref[CODES, i] - 1]
+        return pltpu.make_async_copy(source, held.at[i, heads], load_sems.at[i, k])
+
+    def store(i, heads, k):
+        return pltpu.make_async_copy(held.at[i, heads], out_ref.at[i, heads], store_sems.at[i, k])
+
+    def forward(piece):
+        load(*piece).wait()
+        store(*piece).start()
+
+    for piece in pieces:
+        pl.when(table_ref[CODES, piece[0]] > 0)(lambda piece=piece: load(*piece).start())
+    for piece in pieces:
+        pl.when(table_ref[CODES, piece[0]] > 0)(lambda piece=piece: forward(piece))
+    for piece in pieces:
+        pl.when(table_ref[CODES, piece[0]] > 0)(lambda piece=piece: store(*piece).wait())
 
 
 def grow_kernel(
@@ -339,8 +341,8 @@
         out_specs=anywhere,
         scratch_shapes=[
             pltpu.VMEM(blocks.shape, dtype),
-            pltpu.SemaphoreType.DMA((group_count,)),
-            pltpu.SemaphoreType.DMA((group_count,)),
+            pltpu.SemaphoreType.DMA((group_count, math.gcd(kv_heads, 4))),
+            pltpu.SemaphoreType.DMA((group_count, math.gcd(kv_heads, 4))),
         ],
         out_shape=blocks,
         compiler_params=pltpu.CompilerParams(vmem_limit_bytes=VMEM_LIMIT),

time: 229 us -> 231 us (level)
  Pallas kernels: 54.3 us -> 88.7 us
  waiting for transfers between devices: 59.7 us -> 27.2 us
    all_to_all x1, waiting for transfers between devices: 59.7 us -> 27.2 us  [local(): lax.all_to_all(leaving, ('tp', 'grp'), split_axis=0, concat_axis=0, tiled...]
    pallas_call x1, Pallas kernels: 41.1 us -> 73.6 us  [local(): pl.pallas_call(attend_kernel, in_specs=[smem, vmem, vmem, anywhere], out_...]
  transfers between devices with their start and end apart: 1 -> 1, of which waited for: 1 -> 1; matrix products, arithmetic and copies ran while one was open for 0% -> 0% of each run, Pallas kernels for 18% -> 32%
where the time goes in v7:
time: 231 us
  blocking collectives  109 us (47%)
  Pallas kernels  88.7 us (38%)
  waiting for transfers between devices  27.2 us (12%)
  starting transfers between devices  4.88 us (2%)
    all_to_all x1, blocking collectives, local(): lax.all_to_all(outgoing.reshape(rows.shape), ('tp', 'grp'), split_axis=0,...  109 us
    pallas_call x1, Pallas kernels, local(): pl.pallas_call(attend_kernel, in_specs=[smem, vmem, vmem, anywhere], out_...  73.6 us
    all_to_all x1, waiting for transfers between devices, local(): lax.all_to_all(leaving, ('tp', 'grp'), split_axis=0, concat_axis=0, tiled...  27.2 us
    pallas_call x1, Pallas kernels, local(): pl.pallas_call(unpack_kernel, in_specs=[smem, anywhere, anywhere], out_sp...  7.24 us
    all_to_all x1, starting transfers between devices, local(): lax.all_to_all(leaving, ('tp', 'grp'), split_axis=0, concat_axis=0, tiled...  4.88 us
  transfers between devices with their start and end apart: 1, of which 1 were waited for; matrix products, arithmetic and copies ran while one was open for 0% of the time, Pallas kernels for 32%

profile of v7, /device:TPU:1, one launch (start us, length us, event | category | flops | bytes accessed | tf_op | source)
XLA Modules:
  0.0 230.6 jit_solution(12677077362616803330)
XLA Ops:
  0.6 3.8 %pack.1 = (bf16[8,16,128,256]{3,2,1,0:T(8,128)(2,1)S(1)}, s32[8,128]{1,0:T(8,128)}) custom-call(s32[32]{0:T(128)} %seat_ref.1, s32[32]{0:T(128)} %lens_ref.1, s32[32,64]{1,0:T(8,128)} %old_ref.1, s32[32,64]{1,0:T(8,128)} %new_ref.1, bf16[16,8,128,256]{3,2,1,0:T(8,128)(2,1)} %pool_ref.1), custom_call_target="tpu_custom_call" | custom-call | tf_op jit(solution)/shard_map/pack/pallas_call | solution.py:287
  4.4 0.0 copy-start
  4.5 0.0 copy-start.1
  4.5 109.1 %all_to_all.10.recv_ref = bf16[128,128,256]{2,1,0:T(8,128)(2,1)S(1)} all-to-all(bf16[128,128,256]{2,1,0:T(8,128)(2,1)S(1)} %bitcast.3), channel_id=1, replica_groups=mesh['grp'=16,'tp'=8] {'tp','grp'}, dimensions={0} | all-to-all | bytes 16777216 | tf_op jit(solution)/shard_map/all_to_all | solution.py:296
  113.6 0.0 copy-done
  113.6 0.0 copy-done.1
  113.6 4.0 %grow.1.grown_ref = bf16[128,128,256]{2,1,0:T(8,128)(2,1)} custom-call(s32[8,128]{1,0:T(8,128)S(1)} %copy-done.1, bf16[2,256,256]{2,1,0:T(8,128)(2,1)S(1)} %bitcast.5, bf16[128,128,256]{2,1,0:T(8,128)(2,1)S(1)} %all_to_all.10.recv_ref), custom_call_target="tpu_custom_call" | custom-call | tf_op jit(solution)/shard_map/grow/pallas_call | solution.py:300
  117.6 4.9 %all-to-all-start.1 = ((bf16[128,128,256]{2,1,0:T(8,128)(2,1)}), bf16[128,128,256]{2,1,0:T(8,128)(2,1)}, u32[]{:S(2)}, u32[]{:S(2)}) async-start(bf16[128,128,256]{2,1,0:T(8,128)(2,1)} %grow.1.grown_ref), calls=%async_computation.1 | async-start | bytes 16777216 | tf_op jit(solution)/shard_map/all_to_all | solution.py:314
  122.5 73.6 %attend.1 = (bf16[2,8,256,128]{3,2,1,0:T(8,128)(2,1)}, bf16[16,8,128,256]{3,2,1,0:T(8,128)(2,1)}) custom-call(s32[8,128]{1,0:T(8,128)} %get-tuple-element.6.table_ref, bf16[2,8,256,128]{3,2,1,0:T(8,128)(2,1)} %queries_ref.1, bf16[2,256,256]{2,1,0:T(8,128)(2,1)} %bitcast.4, bf16[128,128,256]{2,1,0:T(8,128)(2,1)} %grow.1.grown_ref), custom_call_target="tpu_custom_call" | custom-call | flops 17179869184 | bytes 8388608 | tf_op jit(solution)/shard_map/attend/pallas_call | solution.py:316
  196.1 27.2 %all-to-all-done.1 = bf16[128,128,256]{2,1,0:T(8,128)(2,1)} async-done(((bf16[128,128,256]{2,1,0:T(8,128)(2,1)}), bf16[128,128,256]{2,1,0:T(8,128)(2,1)}, u32[]{:S(2)}, u32[]{:S(2)}) %all-to-all-start.1) | async-done | bytes 8388640 | tf_op jit(solution)/shard_map/all_to_all | solution.py:314
  223.3 7.2 %unpack.1 = bf16[16,8,128,256]{3,2,1,0:T(8,128)(2,1)} custom-call(s32[8,128]{1,0:T(8,128)} %get-tuple-element.6.table_ref, bf16[8,16,128,256]{3,2,1,0:T(8,128)(2,1)} %bitcast.2.arrived_ref, bf16[16,8,128,256]{3,2,1,0:T(8,128)(2,1)} %get-tuple-element.9.cleared_ref), custom_call_target="tpu_custom_call", output_to_operand_aliasing={{}: (2, {})} | custom-call | tf_op jit(solution)/shard_map/unpack/pallas_call | solution.py:338
Async XLA Ops:
  4.4 109.1 %copy-start = (bf16[2,1,256,256]{3,2,1,0:T(8,128)(2,1)S(1)}, bf16[2,1,256,256]{3,2,1,0:T(8,128)(2,1)}, u32[]{:S(2)}) copy-start(bf16[2,1,256,256]{3,2,1,0:T(8,128)(2,1)} %param.8) | copy-start | bytes 786436
  4.5 109.1 %copy-start.1 = (s32[8,128]{1,0:T(8,128)S(1)}, s32[8,128]{1,0:T(8,128)}, u32[]{:S(2)}) copy-start(s32[8,128]{1,0:T(8,128)} %get-tuple-element.6.table_ref) | copy-start | bytes 12292
  117.6 105.7 %all-to-all-start.1 = ((bf16[128,128,256]{2,1,0:T(8,128)(2,1)}), bf16[128,128,256]{2,1,0:T(8,128)(2,1)}, u32[]{:S(2)}, u32[]{:S(2)}) async-start(bf16[128,128,256]{2,1,0:T(8,128)(2,1)} %grow.1.grown_ref), calls=%async_computation.1 | async-start | bytes 16777216 | tf_op jit(solution)/shard_map/all_to_all | solution.py:314
